TPU v7x, 32 devices: a whole 2x2x4 slice. The times are simulated.
32 devices in a mesh: tm: 2 (over y), chan: 16 (over z, x, core).
Axes of the slice: x: 2, y: 2, z: 4, core: 2. Of those that a mesh axis runs over, the one named last changes fastest.
Arguments:
- record: bfloat16 [8192, 8192], P('chan', 'tm'), may hold values from -6 to 6
- fan_mask: int32 [256, 8192], P('chan'), may hold values 0 or 1
Outputs:
- filtered: float32 [8192, 8192], P('chan', 'tm')
All inputs are finite; a program needn't handle non-finite values. No bound on the sum of `fan_mask` on one device may be relied on, other than what follows from the above.
Results may differ from a plain program's by a relative error of at most 0.0084.
Values may be sent and summed in bfloat16 or wider, within the bound.
A program may use at most 128 MiB of HBM per device.

v0:
```python
import math

import jax
import jax.numpy as jnp
from jax import lax
from jax.sharding import PartitionSpec as P

NCH = 8192
SECTION_A = 64
WIN = 512
SECTION_B = 128
HOP = 256
BINS = 256


def passed_along(value, axis, by):
    peers = lax.axis_size(axis)
    pairs = [(i, i + by) for i in range(peers) if 0 <= i + by < peers]
    return lax.ppermute(value, axis, pairs)


def hann_taper(length):
    steps = jnp.arange(length, dtype=jnp.int32).astype(jnp.float32)
    return 0.5 - 0.5 * jnp.cos(steps * (2.0 * math.pi / length))


def time_table(length, bins):
    rows = jnp.arange(length, dtype=jnp.int32)[:, None]
    cols = jnp.arange(bins, dtype=jnp.int32)[None, :]
    phase = (rows * cols % length).astype(jnp.float32) * (2.0 * math.pi / length)
    return jnp.concatenate([jnp.cos(phase), -jnp.sin(phase)], axis=1).astype(jnp.bfloat16)


def inverse_time_table(length, bins):
    rows = jnp.arange(bins, dtype=jnp.int32)[:, None]
    cols = jnp.arange(length, dtype=jnp.int32)[None, :]
    phase = (rows * cols % length).astype(jnp.float32) * (2.0 * math.pi / length)
    weight = jnp.where(rows == 0, 1.0, 2.0).astype(jnp.float32) / length
    return jnp.stack([weight * jnp.cos(phase), -weight * jnp.sin(phase)]).astype(jnp.bfloat16)


def block_table(order_len, exponent_sign):
    rows = jnp.arange(order_len, dtype=jnp.int32)[:, None]
    cols = jnp.arange(order_len, dtype=jnp.int32)[None, :]
    phase = (rows * cols % order_len).astype(jnp.float32) * (2.0 * math.pi / order_len)
    cosine = jnp.cos(phase)
    sine = exponent_sign * jnp.sin(phase)
    real_row = jnp.stack([cosine, sine], axis=1)
    imag_row = jnp.stack([-sine, cosine], axis=1)
    return jnp.stack([real_row, imag_row], axis=0).astype(jnp.bfloat16)


def twiddle_pair(row_count, col_count, total, exponent_sign):
    rows = jnp.arange(row_count, dtype=jnp.int32)[:, None]
    cols = jnp.arange(col_count, dtype=jnp.int32)[None, :]
    phase = (rows * cols % total).astype(jnp.float32) * (2.0 * math.pi / total)
    return (jnp.cos(phase), exponent_sign * jnp.sin(phase))


def rotate(values, cosine, sine):
    return jnp.stack([values[0] * cosine - values[1] * sine, values[0] * sine + values[1] * cosine])


def body(record, fan_mask):
    channels, span_len = record.shape
    frames_here = span_len // HOP
    taper = hann_taper(WIN)
    forward_time = time_table(WIN, BINS).T
    inverse_time = inverse_time_table(WIN, BINS)
    outer_fwd = block_table(SECTION_A, -1.0)
    inner_fwd = block_table(SECTION_B, -1.0)
    inner_inv = block_table(SECTION_B, 1.0)
    outer_inv = block_table(SECTION_A, 1.0)
    fwd_cos, fwd_sin = twiddle_pair(SECTION_A, SECTION_B, NCH, -1.0)
    inv_cos, inv_sin = twiddle_pair(SECTION_A, SECTION_B, NCH, 1.0)
    fwd_cos = fwd_cos[:, None, None, :]
    fwd_sin = fwd_sin[:, None, None, :]
    inv_cos = inv_cos[:, None, None, :]
    inv_sin = inv_sin[:, None, None, :]
    local_bins = fan_mask.shape[0]
    fk_gate = (
        fan_mask.reshape(local_bins, SECTION_B, SECTION_A).transpose(2, 0, 1).astype(jnp.float32)
    )
    fk_gate = fk_gate[:, :, None, None, :]
    time_major = record.T
    rim_rows = passed_along(time_major[:HOP], "tm", -1)
    extended = jnp.concatenate([time_major, rim_rows], axis=0)
    blocks = extended.reshape(frames_here + 1, HOP, channels).astype(jnp.float32)
    first_half = (blocks[:-1] * taper[:HOP, None]).astype(jnp.bfloat16)
    second_half = (blocks[1:] * taper[HOP:, None]).astype(jnp.bfloat16)
    spectra = jnp.einsum(
        "jn,fnc->jfc", forward_time[:, :HOP], first_half, preferred_element_type=jnp.float32
    )
    spectra = spectra + jnp.einsum(
        "jn,fnc->jfc", forward_time[:, HOP:], second_half, preferred_element_type=jnp.float32
    )
    spectra = spectra.astype(jnp.bfloat16).reshape(2, BINS, frames_here, channels)
    bin_grid = lax.all_to_all(spectra, "chan", split_axis=1, concat_axis=3, tiled=True)
    bin_count = bin_grid.shape[1]
    item_count = bin_grid.shape[2]
    split_grid = bin_grid.reshape(2, bin_count, item_count, SECTION_A, SECTION_B)
    section_one = jnp.einsum(
        "ipoj,ikfpq->ojkfq", outer_fwd, split_grid, preferred_element_type=jnp.float32
    )
    section_one = rotate(section_one, fwd_cos, fwd_sin).astype(jnp.bfloat16)
    fk_plane = jnp.einsum(
        "ijkfq,iqor->jkfor", section_one, inner_fwd, preferred_element_type=jnp.float32
    )
    fk_plane = (fk_plane * fk_gate).astype(jnp.bfloat16)
    section_three = jnp.einsum(
        "jkfir,iroq->jkfoq", fk_plane, inner_inv, preferred_element_type=jnp.float32
    )
    real_part = section_three[:, :, :, 0]
    imag_part = section_three[:, :, :, 1]
    section_three = jnp.stack(
        [real_part * inv_cos - imag_part * inv_sin, real_part * inv_sin + imag_part * inv_cos]
    ).astype(jnp.bfloat16)
    restored = jnp.einsum(
        "ijkfq,ijop->opkfq", section_three, outer_inv, preferred_element_type=jnp.float32
    )
    restored = (restored * (1.0 / NCH)).astype(jnp.bfloat16)
    restored = restored.transpose(0, 2, 3, 1, 4).reshape(2, bin_count, item_count, NCH)
    returned = lax.all_to_all(restored, "chan", split_axis=3, concat_axis=1, tiled=True)
    signal = jnp.einsum("ikn,ikfc->nfc", inverse_time, returned, preferred_element_type=jnp.float32)
    head_half = signal[:HOP]
    tail_half = signal[HOP:]
    carried = passed_along(tail_half[:, -1].astype(jnp.bfloat16), "tm", 1).astype(jnp.float32)
    output_blocks = head_half + jnp.concatenate([carried[:, None], tail_half[:, :-1]], axis=1)
    return output_blocks.transpose(2, 1, 0).reshape(channels, span_len)


def solution(mesh):
    placed = (P("chan", "tm"), P("chan", None))
    return jax.shard_map(
        body, mesh=mesh, in_specs=placed, out_specs=P("chan", "tm"), check_vma=False
    )
```

profile of v0, /device:TPU:15, one launch (start us, length us, event | category | flops | bytes accessed | tf_op | source)
XLA Modules:
  0.0 810.5 jit_solution(17757031560539121104)
XLA Ops:
  1.0 2.1 collective-permute-start
  3.1 2.2 negate_convert_fusion
  5.4 2.7 collective-permute-done
  8.1 2.9 maximum_convert_fusion
  11.0 7.1 fusion.78
  18.1 9.0 %copy.56 = f32[4096,512]{1,0:T(8,128)} copy(f32[4096,512]{0,1:T(8,128)} %get-tuple-element.10) | data formatting | bytes 16777216 | tf_op jit(solution)/shard_map/slice | solution.py:89
  27.1 9.0 %copy.57 = f32[4096,512]{1,0:T(8,128)} copy(f32[4096,512]{0,1:T(8,128)} %get-tuple-element.9) | data formatting | bytes 16777216 | tf_op jit(solution)/shard_map/slice | solution.py:90
  36.2 11.5 %fusion.17 = f32[512,16,512]{2,0,1:T(8,128)} fusion(f32[16,256,512]{2,1,0:T(8,128)} %bitcast.130, f32[256]{0:T(256)S(1)} %get-tuple-element.20, bf16[512,512]{1,0:T(8,128)(2,1)S(1)} %maximum_bitcast_fusion.3), kind=kOutput, calls=%fused_computation.29 | convolution fusion | flops 2151677952 | bytes 25428992 | tf_op jit(solution)/shard_map/jn,fnc->jfc/dot_general | solution.py:91
  47.7 14.1 %add_convert_fusion = bf16[512,16,512]{2,0,1:T(8,128)(2,1)} fusion(f32[512,16,512]{2,0,1:T(8,128)} %fusion.17, f32[16,256,512]{2,1,0:T(8,128)} %bitcast.127, f32[256]{0:T(256)S(1)} %get-tuple-element.19, bf16[512,512]{1,0:T(8,128)(2,1)S(1)} %maximum_bitcast_fusion.3), kind=kOutput, calls=%fused_computation.4 | convolution fusion | flops 2160066560 | bytes 33817600 | tf_op jit(solution)/shard_map/jn,fnc->jfc/dot_general | solution.py:94
  61.8 16.4 %copy.30 = bf16[2,256,16,512]{3,0,2,1:T(2,128)(2,1)} copy(bf16[2,256,16,512]{3,1,0,2:T(8,128)(2,1)} %bitcast.128) | data formatting | bytes 16777216 | tf_op jit(solution)/shard_map/reshape | solution.py:97
  78.2 7.7 all-to-all-start
  88.4 179.7 %all-to-all-done = bf16[2,256,16,512]{3,0,2,1:T(2,128)(2,1)} async-done(((bf16[2,256,16,512]{3,0,2,1:T(2,128)(2,1)}), bf16[2,256,16,512]{3,0,2,1:T(2,128)(2,1)}, u32[]{:S(2)}, u32[]{:S(2)}) %all-to-all-start) | async-done | bytes 8388640 | tf_op jit(solution)/shard_map/all_to_all | solution.py:98
  268.1 16.6 %copy.84 = bf16[2,16,16,16,512]{4,1,0,3,2:T(8,128)(2,1)} copy(bf16[2,16,16,16,512]{4,0,3,2,1:T(2,128)(2,1)} %bitcast.16) | data formatting | bytes 16777216 | tf_op jit(solution)/shard_map/all_to_all | solution.py:98
  284.7 13.9 %reshape.430 = bf16[2,16,16,64,128,1]{4,3,0,2,1,5:T(8,128)(2,1)} reshape(bf16[2,16,16,16,512]{4,3,0,2,1:T(8,128)(2,1)} %bitcast.131) | data formatting | bytes 16777216 | tf_op jit(solution)/shard_map/reshape | solution.py:101
  298.7 5.8 convolution_bitcast_fusion.1
  304.4 3.9 subtract_convert_fusion.1
  308.3 6.3 maximum_bitcast_fusion
  314.7 24.8 %fusion.14 = bf16[64,16,16,2,128,1]{4,2,3,1,0,5:T(8,128)(2,1)} fusion(f32[64,16,128]{2,1,0:T(8,128)S(1)} %copy.34, bf16[2,64,16,16,128,1]{4,1,3,2,0,5:T(8,128)(2,1)} %maximum_bitcast_fusion, bf16[1,128,2,128]{3,1,0,2:T(8,128)(2,1)S(1)} %get-tuple-element.13, bf16[1,128,2,128]{3,1,0,2:T(8,128)(2,1)S(1)} %get-tuple-element.14), kind=kOutput, calls=%fused_computation.27 | convolution fusion | flops 2156134400 | bytes 17432576 | tf_op jit(solution)/shard_map/ijkfq,iqor->jkfor/dot_general | solution.py:106
  339.4 9.4 %fusion.9 = f32[64,16,16,2,128]{4,0,2,1,3:T(8,128)S(1)} fusion(bf16[64,16,16,2,128,1]{4,2,3,1,0,5:T(8,128)(2,1)} %fusion.14, bf16[1,128,2,128]{3,1,2,0:T(8,128)(2,1)S(1)} %get-tuple-element.12, bf16[1,128,2,128]{3,1,2,0:T(8,128)(2,1)S(1)} %get-tuple-element.11), kind=kOutput, calls=%fused_computation.25 | convolution fusion | flops 2147549184 | bytes 25296896 | tf_op jit(solution)/shard_map/jkfir,iroq->jkfoq/dot_general | solution.py:110
  348.8 2.5 subtract_convert_fusion
  351.3 4.7 fusion.2
  356.1 45.4 %copy.64 = bf16[2,16,16,64,128]{2,1,0,4,3:T(8,128)(2,1)} copy(bf16[2,16,16,64,128]{4,3,2,1,0:T(8,128)(2,1)} %fusion.2) | data formatting | bytes 16777216 | tf_op jit(solution)/shard_map/reshape | solution.py:122
  401.5 72.4 %reshape.444 = bf16[16,2,131072]{2,1,0:T(2,128)(2,1)} reshape(bf16[8192,2,16,16]{3,2,1,0:T(8,128)(2,1)} %bitcast.117) | data formatting | bytes 16777216
  473.9 5.3 all-to-all-start.1
  479.2 2.2 multiply_convert_fusion.4
  481.4 179.9 %all-to-all-done.1 = bf16[16,2,131072]{2,1,0:T(2,128)(2,1)} async-done(((bf16[16,2,131072]{2,1,0:T(2,128)(2,1)}), bf16[16,2,131072]{2,1,0:T(2,128)(2,1)}, u32[]{:S(2)}, u32[]{:S(2)}) %all-to-all-start.1) | async-done | bytes 8388640 | tf_op jit(solution)/shard_map/all_to_all | solution.py:123
  661.3 48.5 %reshape.445 = bf16[8192,2,16,16]{3,2,1,0:T(8,128)(2,1)} reshape(bf16[16,2,131072]{2,1,0:T(2,128)(2,1)} %all-to-all-done.1) | data formatting | bytes 16777216
  709.9 69.9 %copy.41 = bf16[2,16,16,16,512]{4,1,3,0,2:T(8,128)(2,1)} copy(bf16[2,16,16,16,512]{2,1,0,4,3:T(8,128)(2,1)} %bitcast.43) | data formatting | bytes 16777216 | tf_op jit(solution)/shard_map/all_to_all | solution.py:123
  779.8 7.2 convolution_bitcast_fusion
  789.7 7.3 collective-permute-done.1
  797.0 4.4 slice_add_fusion
  801.4 8.9 %copy.42 = f32[512,4096]{1,0:T(8,128)} copy(f32[512,4096]{0,1:T(8,128)} %bitcast.129) | data formatting | bytes 16777216 | tf_op jit(solution)/shard_map/reshape | solution.py:129
  (25 shorter events, 6.1 us)
Async XLA Ops:
  1.0 7.1 collective-permute-start
  78.2 7.7 copy-start
  78.2 189.9 %all-to-all-start = ((bf16[2,256,16,512]{3,0,2,1:T(2,128)(2,1)}), bf16[2,256,16,512]{3,0,2,1:T(2,128)(2,1)}, u32[]{:S(2)}, u32[]{:S(2)}) async-start(bf16[2,256,16,512]{3,0,2,1:T(2,128)(2,1)} %copy.30), calls=%async_computation | async-start | bytes 16777216 | tf_op jit(solution)/shard_map/all_to_all | solution.py:98
  473.9 187.5 %all-to-all-start.1 = ((bf16[16,2,131072]{2,1,0:T(2,128)(2,1)}), bf16[16,2,131072]{2,1,0:T(2,128)(2,1)}, u32[]{:S(2)}, u32[]{:S(2)}) async-start(bf16[16,2,131072]{2,1,0:T(2,128)(2,1)} %reshape.444), calls=%async_computation.1 | async-start | bytes 16777216 | tf_op jit(solution)/shard_map/all_to_all | solution.py:123
  787.1 9.9 %collective-permute-start.1 = (bf16[256,512]{1,0:T(8,128)(2,1)S(1)}, bf16[256,512]{1,0:T(8,128)(2,1)S(1)}, u32[]{:S(2)}, u32[]{:S(2)}) collective-permute-start(bf16[256,512]{1,0:T(8,128)(2,1)S(1)} %fusion.34), channel_id=1, source_target_pairs={{0,16},{1,17},{2,18},{3,19},{4,20},{5,21},{6,22},{7,23},{8,24},{9,... | collective-permute-start | bytes 786440 | tf_op jit(solution)/shard_map/ppermute | solution.py:19
where the time goes:
time: 820 us; the launch traced here: 811 us
  waiting for transfers between devices  370 us (45%)
  local copies, waits for them, and re-layouts  320 us (39%)
  matrix products  77.5 us (9%)
  other arithmetic  26.2 us (3%)
  starting transfers between devices  16.4 us (2%)
    all_to_all x1, waiting for transfers between devices, body(): lax.all_to_all(restored, 'chan', split_axis=3, concat_axis=1, tiled=True)  180 us
    all_to_all x1, waiting for transfers between devices, body(): lax.all_to_all(spectra, 'chan', split_axis=1, concat_axis=3, tiled=True)  180 us
    unnamed x4, local copies, waits for them, and re-layouts  121 us
    all_to_all x1, local copies, waits for them, and re-layouts, body(): lax.all_to_all(restored, 'chan', split_axis=3, concat_axis=1, tiled=True)  69.9 us
    reshape x1, local copies, waits for them, and re-layouts, body(): restored.transpose(0, 2, 3, 1, 4).reshape(2, bin_count, item_count, NCH)  45.4 us
    dot_general x1, matrix products, body(): jnp.einsum('ijkfq,iqor->jkfor', section_one, inner_fwd, preferred_element...  24.8 us
    all_to_all x1, local copies, waits for them, and re-layouts, body(): lax.all_to_all(spectra, 'chan', split_axis=1, concat_axis=3, tiled=True)  16.6 us
  transfers between devices with their start and end apart: 4, of which 4 were waited for; matrix products, arithmetic and copies ran while one was open for 1% of the time, Pallas kernels for 0%

commit v1 on v0

--- a/solution.py
+++ b/solution.py
@@ -1,8 +1,11 @@
+import functools
 import math
 
 import jax
 import jax.numpy as jnp
 from jax import lax
+from jax.experimental import pallas as pl
+from jax.experimental.pallas import tpu as pltpu
 from jax.sharding import PartitionSpec as P
 
 NCH = 8192
@@ -61,7 +64,7 @@
     return jnp.stack([values[0] * cosine - values[1] * sine, values[0] * sine + values[1] * cosine])
 
 
-def body(record, fan_mask):
+def bins_body(record, fan_mask):
     channels, span_len = record.shape
     frames_here = span_len // HOP
     taper = hann_taper(WIN)
@@ -129,6 +132,197 @@
     return output_blocks.transpose(2, 1, 0).reshape(channels, span_len)
 
 
+LANES = 128
+GROUP = 4
+
+
+def flat_table(order_len, exponent_sign):
+    table = block_table(order_len, exponent_sign)
+    return table.transpose(2, 3, 0, 1).reshape(2 * order_len, 2 * order_len)
+
+
+def frame_kernel(
+    first, second, taper, fwd_time, inv_time, w_one, w_two, w_three, w_four,
+    tw_cos, tw_sin, gate, head, tail, by_q, by_j, restored,
+):
+    def rows_at(index, size):
+        return pl.ds(pl.multiple_of(index * size, size), size)
+
+    parts = fwd_time.shape[0]
+    for part in range(parts):
+        lanes = slice(part * LANES, (part + 1) * LANES)
+
+        @pl.loop(0, SECTION_A // GROUP)
+        def _(step):
+            rows = rows_at(step, GROUP * SECTION_B)
+            left = (first[rows, :].astype(jnp.float32) * taper[:, :HOP]).astype(jnp.bfloat16)
+            right = (second[rows, :].astype(jnp.float32) * taper[:, HOP:]).astype(jnp.bfloat16)
+            spectra = jnp.dot(left, fwd_time[part, :HOP], preferred_element_type=jnp.float32)
+            spectra += jnp.dot(right, fwd_time[part, HOP:], preferred_element_type=jnp.float32)
+            for g in range(GROUP):
+                for i in range(2):
+                    by_q[i, pl.ds(step * GROUP + g, SECTION_B, stride=SECTION_A), :] = spectra[
+                        g * SECTION_B : (g + 1) * SECTION_B, i * LANES : (i + 1) * LANES
+                    ]
+
+        @pl.loop(0, SECTION_B // GROUP)
+        def _(step):
+            columns = []
+            for g in range(GROUP):
+                rows = rows_at(step * GROUP + g, SECTION_A)
+                columns.append(
+                    jnp.concatenate([by_q[0, rows, :], by_q[1, rows, :]], axis=0).astype(jnp.bfloat16)
+                )
+            total = jnp.dot(
+                w_one[...], jnp.concatenate(columns, axis=1), preferred_element_type=jnp.float32
+            )
+            for g in range(GROUP):
+                rows = rows_at(step * GROUP + g, SECTION_A)
+                cosine, sine = tw_cos[rows, :], tw_sin[rows, :]
+                real = total[:SECTION_A, g * LANES : (g + 1) * LANES]
+                imag = total[SECTION_A:, g * LANES : (g + 1) * LANES]
+                spread = pl.ds(step * GROUP + g, SECTION_A, stride=SECTION_B)
+                by_j[0, spread, :] = real * cosine + imag * sine
+                by_j[1, spread, :] = imag * cosine - real * sine
+
+        @pl.loop(0, SECTION_A // GROUP)
+        def _(step):
+            columns, gates = [], []
+            for g in range(GROUP):
+                rows = rows_at(step * GROUP + g, SECTION_B)
+                columns.append(
+                    jnp.concatenate([by_j[0, rows, :], by_j[1, rows, :]], axis=0).astype(jnp.bfloat16)
+                )
+                gates.append(gate[rows, lanes].astype(jnp.float32))
+            plane = jnp.dot(
+                w_two[...], jnp.concatenate(columns, axis=1), preferred_element_type=jnp.float32
+            )
+            passing = jnp.concatenate(gates, axis=1)
+            plane = plane * jnp.concatenate([passing, passing], axis=0)
+            total = jnp.dot(
+                w_three[...], plane.astype(jnp.bfloat16), preferred_element_type=jnp.float32
+            )
+            for g in range(GROUP):
+                spread = pl.ds(step * GROUP + g, SECTION_B, stride=SECTION_A)
+                for i in range(2):
+                    by_q[i, spread, :] = total[
+                        i * SECTION_B : (i + 1) * SECTION_B, g * LANES : (g + 1) * LANES
+                    ]
+
+        @pl.loop(0, SECTION_B // GROUP)
+        def _(step):
+            columns = []
+            for g in range(GROUP):
+                rows = rows_at(step * GROUP + g, SECTION_A)
+                cosine, sine = tw_cos[rows, :], tw_sin[rows, :]
+                real, imag = by_q[0, rows, :], by_q[1, rows, :]
+                columns.append(
+                    jnp.concatenate(
+                        [real * cosine - imag * sine, real * sine + imag * cosine], axis=0
+                    ).astype(jnp.bfloat16)
+                )
+            total = jnp.dot(
+                w_four[...], jnp.concatenate(columns, axis=1), preferred_element_type=jnp.float32
+            ) * (1.0 / NCH)
+            for g in range(GROUP):
+                spread = pl.ds(step * GROUP + g, SECTION_A, stride=SECTION_B)
+                for i in range(2):
+                    by_j[i, spread, :] = total[
+                        i * SECTION_A : (i + 1) * SECTION_A, g * LANES : (g + 1) * LANES
+                    ]
+
+        @pl.loop(0, SECTION_A // GROUP)
+        def _(step):
+            rows = rows_at(step, GROUP * SECTION_B)
+            for i in range(2):
+                at = (2 * part + i) * LANES
+                restored[rows, at : at + LANES] = by_j[i, rows, :].astype(jnp.bfloat16)
+
+    @pl.loop(0, SECTION_A // GROUP)
+    def _(step):
+        rows = rows_at(step, GROUP * SECTION_B)
+        signal = jnp.dot(restored[rows, :], inv_time[...], preferred_element_type=jnp.float32)
+        head[rows, :] = signal[:, :HOP].astype(head.dtype)
+        tail[rows, :] = signal[:, HOP:].astype(tail.dtype)
+
+
+def frame_tables():
+    parts = BINS // LANES
+    fwd_time = time_table(WIN, BINS).reshape(WIN, 2, parts, LANES)
+    fwd_time = fwd_time.transpose(2, 0, 1, 3).reshape(parts, WIN, 2 * LANES)
+    inv_time = inverse_time_table(WIN, BINS).reshape(2, parts, LANES, WIN)
+    inv_time = inv_time.transpose(1, 0, 2, 3).reshape(2 * BINS, WIN)
+    tw_cos, tw_sin = twiddle_pair(SECTION_B, SECTION_A, NCH, 1.0)
+    spread = (SECTION_B, SECTION_A, LANES)
+    return (
+        hann_taper(WIN)[None, :],
+        fwd_time,
+        inv_time,
+        flat_table(SECTION_A, -1.0),
+        flat_table(SECTION_B, -1.0),
+        flat_table(SECTION_B, 1.0),
+        flat_table(SECTION_A, 1.0),
+        jnp.broadcast_to(tw_cos[:, :, None], spread).reshape(NCH, LANES),
+        jnp.broadcast_to(tw_sin[:, :, None], spread).reshape(NCH, LANES),
+    )
+
+
+def filter_frame(first, second, tables, gate):
+    half = jax.ShapeDtypeStruct((NCH, HOP), jnp.bfloat16)
+    whole = pl.BlockSpec(memory_space=pltpu.VMEM)
+    return pl.pallas_call(
+        frame_kernel,
+        out_shape=(half, half),
+        in_specs=[whole] * (3 + len(tables)),
+        out_specs=(whole, whole),
+        scratch_shapes=[
+            pltpu.VMEM((2, NCH, LANES), jnp.float32),
+            pltpu.VMEM((2, NCH, LANES), jnp.float32),
+            pltpu.VMEM((NCH, 2 * BINS), jnp.bfloat16),
+        ],
+        compiler_params=pltpu.CompilerParams(vmem_limit_bytes=60 * 1024 * 1024),
+        cost_estimate=pl.CostEstimate(
+            flops=16_000_000_000, bytes_accessed=30_000_000, transcendentals=0
+        ),
+    )(first, second, *tables, gate)
+
+
+def shifted(value, by):
+    axes = ("tm", "chan")
+    peers = lax.axis_size("tm") * lax.axis_size("chan")
+    pairs = [(i, i + by) for i in range(peers) if 0 <= i + by < peers]
+    return lax.ppermute(value, axes, pairs)
+
+
+def frames_body(record, fan_mask):
+    channels, span_len = record.shape
+    local_bins = fan_mask.shape[0]
+    gate = fan_mask.astype(jnp.bfloat16).reshape(local_bins, SECTION_B, SECTION_A)
+    gate = gate.transpose(0, 2, 1).reshape(local_bins, NCH)
+    gate = lax.all_gather(gate, "chan", axis=0, tiled=True).T
+    tables = frame_tables()
+    mine = lax.all_to_all(record, "chan", split_axis=1, concat_axis=0, tiled=True)
+    after = shifted(mine[:, :HOP], -1)
+    held = mine.shape[1] // HOP
+    blocks = [mine[:, f * HOP : (f + 1) * HOP] for f in range(held)] + [after]
+    halves = [filter_frame(blocks[f], blocks[f + 1], tables, gate) for f in range(held)]
+    before = shifted(halves[-1][1], 1)
+    tails = [before] + [halves[f][1] for f in range(held - 1)]
+    sums = [
+        (halves[f][0].astype(jnp.float32) + tails[f].astype(jnp.float32)).astype(jnp.bfloat16)
+        for f in range(held)
+    ]
+    result = sums[0] if held == 1 else jnp.concatenate(sums, axis=1)
+    result = lax.all_to_all(result, "chan", split_axis=0, concat_axis=1, tiled=True)
+    return result.astype(jnp.float32)
+
+
+def body(record, fan_mask):
+    if (record.shape[1] // HOP) % lax.axis_size("chan") == 0:
+        return frames_body(record, fan_mask)
+    return bins_body(record, fan_mask)
+
+
 def solution(mesh):
     placed = (P("chan", "tm"), P("chan", None))
     return jax.shard_map(

time: 820 us -> 467 us (0.57)
  local copies, waits for them, and re-layouts: 320 us -> 25.5 us
  waiting for transfers between devices: 370 us -> 191 us
  Pallas kernels: 0 us -> 109 us
  blocking collectives: 0 us -> 102 us
  matrix products: 77.5 us -> 0 us
  between operations: 0.45 us -> 13.6 us
  other arithmetic: 26.2 us -> 13.9 us
    all_to_all x2 -> x1, waiting for transfers between devices: 360 us -> 116 us  [frames_body(): lax.all_to_all(record, 'chan', split_axis=1, concat_axis=0, tiled=True)]
    unnamed x4 -> x5, local copies, waits for them, and re-layouts: 121 us -> 2.25 us
    pallas_call x0 -> x1, Pallas kernels: none -> 109 us  [filter_frame(): pl.pallas_call(frame_kernel, out_shape=(half, half), in_specs=[whole] * (...]
    all_to_all x0 -> x1, blocking collectives: none -> 102 us  [frames_body(): lax.all_to_all(result, 'chan', split_axis=0, concat_axis=1, tiled=True)]
    reshape x4 -> x3, local copies, waits for them, and re-layouts: 84.6 us -> 1.95 us  [the longest x2 1.41 us: flat_table(): return table.transpose(2, 3, 0, 1).reshape(2 * order_len, 2 * order_len)]
    all_to_all x2 -> x1, local copies, waits for them, and re-layouts: 86.6 us -> 4.62 us  [frames_body(): lax.all_to_all(record, 'chan', split_axis=1, concat_axis=0, tiled=True)]
    dot_general x7 -> x0, matrix products: 77.5 us -> none  [the longest x1 24.8 us: body(): jnp.einsum('ijkfq,iqor->jkfor', section_one, inner_fwd, preferred_element...]
    ppermute x2, waiting for transfers between devices: 9.93 us -> 75.4 us  [shifted(): return lax.ppermute(value, axes, pairs)]
  transfers between devices with their start and end apart: 4 -> 4, of which waited for: 4 -> 3; matrix products, arithmetic and copies ran while one was open for 1% -> 4% of each run, Pallas kernels for 0% -> 0%
where the time goes in v1:
time: 467 us; the launch traced here: 466 us
  waiting for transfers between devices  191 us (41%)
  Pallas kernels  109 us (23%)
  blocking collectives  102 us (22%)
  local copies, waits for them, and re-layouts  25.5 us (5%)
  other arithmetic  13.9 us (3%)
  between operations  13.6 us (3%)
  starting transfers between devices  10.7 us (2%)
    all_to_all x1, waiting for transfers between devices, frames_body(): lax.all_to_all(record, 'chan', split_axis=1, concat_axis=0, tiled=True)  116 us
    pallas_call x1, Pallas kernels, filter_frame(): pl.pallas_call(frame_kernel, out_shape=(half, half), in_specs=[whole] * (...  109 us
    all_to_all x1, blocking collectives, frames_body(): lax.all_to_all(result, 'chan', split_axis=0, concat_axis=1, tiled=True)  102 us
    ppermute x2, waiting for transfers between devices, shifted(): return lax.ppermute(value, axes, pairs)  75.4 us
  transfers between devices with their start and end apart: 4, of which 3 were waited for; matrix products, arithmetic and copies ran while one was open for 4% of the time, Pallas kernels for 0%

profile of v1, /device:TPU:15, one launch (start us, length us, event | category | flops | bytes accessed | tf_op | source)
XLA Modules:
  0.0 465.6 jit_solution(14164226482469863135)
XLA Ops:
  6.5 4.6 copy.52
  11.2 6.7 %all-to-all-start = ((bf16[512,16,256]{2,0,1:T(8,128)(2,1)}), bf16[512,16,256]{2,0,1:T(8,128)(2,1)}, u32[]{:S(2)}, u32[]{:S(2)}) async-start(bf16[512,16,256]{2,0,1:T(8,128)(2,1)} %bitcast.62), calls=%async_computation | async-start | bytes 8388608 | tf_op jit(solution)/shard_map/all_to_all | solution.py:304
  17.9 0.5 reshape.464
  18.5 0.2 copy.38
  18.7 0.9 copy.53
  19.6 116.0 %all-to-all-done = bf16[512,16,256]{2,0,1:T(8,128)(2,1)} async-done(((bf16[512,16,256]{2,0,1:T(8,128)(2,1)}), bf16[512,16,256]{2,0,1:T(8,128)(2,1)}, u32[]{:S(2)}, u32[]{:S(2)}) %all-to-all-start) | async-done | bytes 4194336 | tf_op jit(solution)/shard_map/all_to_all | solution.py:304
  135.6 2.1 collective-permute-start
  138.6 0.7 reshape.460.w_one
  139.5 0.7 reshape.463.w_four
  140.2 0.3 fusion.33
  140.5 0.3 multiply_convert_fusion.2
  140.8 0.3 cosine_convert_fusion.1
  141.0 0.3 negate_convert_fusion.2
  141.3 0.3 negate_convert_fusion.1
  141.8 0.7 copy.55
  142.6 0.7 copy.54
  143.3 0.7 multiply_subtract_fusion.taper
  143.9 2.5 multiply_convert_fusion.1
  146.4 0.9 pad_maximum_fusion
  147.3 2.2 cosine_convert_fusion
  149.5 0.9 copy_bitcast_fusion.1.fwd_time
  150.6 6.4 %copy.39 = bf16[256,8192]{0,1:T(8,128)(2,1)} copy(bf16[256,8192]{1,0:T(8,128)(2,1)} %all-gather.2.cloned.1.call-done) | data formatting | bytes 8388608 | tf_op jit(solution)/shard_map/all_gather | solution.py:302
  157.0 29.6 %collective-permute-done.second = bf16[8192,256]{1,0:T(8,128)(2,1)} collective-permute-done((bf16[8192,256]{1,0:T(8,128)(2,1)}, bf16[8192,256]{1,0:T(8,128)(2,1)}, u32[]{:S(2)}, u32[]{:S(2)}) %collective-permute-start) | collective-permute-done | bytes 4194336 | tf_op jit(solution)/shard_map/ppermute | solution.py:294
  186.6 2.5 broadcast_in_dim.15.tw_sin
  189.2 2.6 broadcast_in_dim.14.tw_cos
  191.8 108.9 %shard_map.28 = (bf16[8192,256]{1,0:T(8,128)(2,1)}, bf16[8192,256]{1,0:T(8,128)(2,1)}) custom-call(bf16[8192,256]{1,0:T(8,128)(2,1)} %bitcast.1.first, bf16[8192,256]{1,0:T(8,128)(2,1)} %collective-permute-done.second, f32[1,512]{1,0:T(1,128)} %multiply_subtract_fusion.taper, bf16[2,512,256]{2,1,0:T(8,128)(2,1)} %copy_bitcast_fusion.1.fwd_time, ...), custom_call_target="tpu_custom_call" | custom-call | flops 16000000000 | bytes 30000000 | tf_op jit(solution)/shard_map/pallas_call | solution.py:273
  300.7 1.9 collective-permute-start.1
  302.6 45.7 %collective-permute-done.1 = bf16[8192,256]{1,0:T(8,128)(2,1)S(1)} collective-permute-done((bf16[8192,256]{1,0:T(8,128)(2,1)}, bf16[8192,256]{1,0:T(8,128)(2,1)S(1)}, u32[]{:S(2)}, u32[]{:S(2)}) %collective-permute-start.1) | collective-permute-done | bytes 4194336 | tf_op jit(solution)/shard_map/ppermute | solution.py:294
  348.4 3.5 add_convert_fusion
  351.9 101.6 %all_to_all.32 = bf16[16,512,256]{2,1,0:T(8,128)(2,1)S(1)} all-to-all(bf16[16,512,256]{2,1,0:T(8,128)(2,1)S(1)} %bitcast.61), channel_id=1, replica_groups=mesh['tm'=2,'chan'=16] {'chan'}, dimensions={0} | all-to-all | bytes 8388608 | tf_op jit(solution)/shard_map/all_to_all | solution.py:316
  453.5 0.9 convert_bitcast_fusion
  454.4 4.4 copy.43
  (24 shorter events, 1.6 us)
Async XLA Ops:
  11.2 6.7 %copy-start = (s32[16,8192]{1,0:T(8,128)S(1)}, s32[16,8192]{1,0:T(8,128)}, u32[]{:S(2)}) copy-start(s32[16,8192]{1,0:T(8,128)} %param.3) | copy-start | bytes 1572868
  11.2 124.4 %all-to-all-start = ((bf16[512,16,256]{2,0,1:T(8,128)(2,1)}), bf16[512,16,256]{2,0,1:T(8,128)(2,1)}, u32[]{:S(2)}, u32[]{:S(2)}) async-start(bf16[512,16,256]{2,0,1:T(8,128)(2,1)} %bitcast.62), calls=%async_computation | async-start | bytes 8388608 | tf_op jit(solution)/shard_map/all_to_all | solution.py:304
  17.8 132.7 %all-gather.2.cloned.1.call-start = ((), (), s32[]{:S(2)}) async-start(), calls=%async_computation.2 | async-start | bytes 4456448 | tf_op jit(solution)/shard_map/all_gather | solution.py:302
  135.6 51.0 %collective-permute-start = (bf16[8192,256]{1,0:T(8,128)(2,1)}, bf16[8192,256]{1,0:T(8,128)(2,1)}, u32[]{:S(2)}, u32[]{:S(2)}) collective-permute-start(bf16[8192,256]{1,0:T(8,128)(2,1)} %bitcast.1.first), channel_id=1, source_target_pairs={{1,0},{2,1},{3,2},{4,3},{5,4},{6,5},{7,6},{8,7},{9,8},{10,9},{11,1... | collective-permute-start | bytes 12582920 | tf_op jit(solution)/shard_map/ppermute | solution.py:294
  300.7 47.7 %collective-permute-start.1 = (bf16[8192,256]{1,0:T(8,128)(2,1)}, bf16[8192,256]{1,0:T(8,128)(2,1)S(1)}, u32[]{:S(2)}, u32[]{:S(2)}) collective-permute-start(bf16[8192,256]{1,0:T(8,128)(2,1)} %get-tuple-element.8), channel_id=1, source_target_pairs={{0,1},{1,2},{2,3},{3,4},{4,5},{5,6},{6,7},{7,8},{8,9},{9,10},{10,1... | collective-permute-start | bytes 12582920 | tf_op jit(solution)/shard_map/ppermute | solution.py:294
Sparse Core Ops, SparseCore 0:
  20.8 94.8 all-gather.1

commit v2 on v1

--- a/solution.py
+++ b/solution.py
@@ -133,7 +133,9 @@
 
 
 LANES = 128
-GROUP = 4
+GROUP = 8
+PITCH_Q = SECTION_A + 1
+PITCH_J = SECTION_B + 1
 
 
 def flat_table(order_len, exponent_sign):
@@ -148,6 +150,9 @@
     def rows_at(index, size):
         return pl.ds(pl.multiple_of(index * size, size), size)
 
+    def padded(step, g, size):
+        return pl.ds(pl.multiple_of(step * (GROUP * (size + 1)), 8) + g * (size + 1), size)
+
     parts = fwd_time.shape[0]
     for part in range(parts):
         lanes = slice(part * LANES, (part + 1) * LANES)
@@ -161,7 +166,7 @@
             spectra += jnp.dot(right, fwd_time[part, HOP:], preferred_element_type=jnp.float32)
             for g in range(GROUP):
                 for i in range(2):
-                    by_q[i, pl.ds(step * GROUP + g, SECTION_B, stride=SECTION_A), :] = spectra[
+                    by_q[i, pl.ds(step * GROUP + g, SECTION_B, stride=PITCH_Q), :] = spectra[
                         g * SECTION_B : (g + 1) * SECTION_B, i * LANES : (i + 1) * LANES
                     ]
 
@@ -169,7 +174,7 @@
         def _(step):
             columns = []
             for g in range(GROUP):
-                rows = rows_at(step * GROUP + g, SECTION_A)
+                rows = padded(step, g, SECTION_A)
                 columns.append(
                     jnp.concatenate([by_q[0, rows, :], by_q[1, rows, :]], axis=0).astype(jnp.bfloat16)
                 )
@@ -181,7 +186,7 @@
                 cosine, sine = tw_cos[rows, :], tw_sin[rows, :]
                 real = total[:SECTION_A, g * LANES : (g + 1) * LANES]
                 imag = total[SECTION_A:, g * LANES : (g + 1) * LANES]
-                spread = pl.ds(step * GROUP + g, SECTION_A, stride=SECTION_B)
+                spread = pl.ds(step * GROUP + g, SECTION_A, stride=PITCH_J)
                 by_j[0, spread, :] = real * cosine + imag * sine
                 by_j[1, spread, :] = imag * cosine - real * sine
 
@@ -190,8 +195,9 @@
             columns, gates = [], []
             for g in range(GROUP):
                 rows = rows_at(step * GROUP + g, SECTION_B)
+                held = padded(step, g, SECTION_B)
                 columns.append(
-                    jnp.concatenate([by_j[0, rows, :], by_j[1, rows, :]], axis=0).astype(jnp.bfloat16)
+                    jnp.concatenate([by_j[0, held, :], by_j[1, held, :]], axis=0).astype(jnp.bfloat16)
                 )
                 gates.append(gate[rows, lanes].astype(jnp.float32))
             plane = jnp.dot(
@@ -203,7 +209,7 @@
                 w_three[...], plane.astype(jnp.bfloat16), preferred_element_type=jnp.float32
             )
             for g in range(GROUP):
-                spread = pl.ds(step * GROUP + g, SECTION_B, stride=SECTION_A)
+                spread = pl.ds(step * GROUP + g, SECTION_B, stride=PITCH_Q)
                 for i in range(2):
                     by_q[i, spread, :] = total[
                         i * SECTION_B : (i + 1) * SECTION_B, g * LANES : (g + 1) * LANES
@@ -215,7 +221,8 @@
             for g in range(GROUP):
                 rows = rows_at(step * GROUP + g, SECTION_A)
                 cosine, sine = tw_cos[rows, :], tw_sin[rows, :]
-                real, imag = by_q[0, rows, :], by_q[1, rows, :]
+                held = padded(step, g, SECTION_A)
+                real, imag = by_q[0, held, :], by_q[1, held, :]
                 columns.append(
                     jnp.concatenate(
                         [real * cosine - imag * sine, real * sine + imag * cosine], axis=0
@@ -225,7 +232,7 @@
                 w_four[...], jnp.concatenate(columns, axis=1), preferred_element_type=jnp.float32
             ) * (1.0 / NCH)
             for g in range(GROUP):
-                spread = pl.ds(step * GROUP + g, SECTION_A, stride=SECTION_B)
+                spread = pl.ds(step * GROUP + g, SECTION_A, stride=PITCH_J)
                 for i in range(2):
                     by_j[i, spread, :] = total[
                         i * SECTION_A : (i + 1) * SECTION_A, g * LANES : (g + 1) * LANES
@@ -233,10 +240,13 @@
 
         @pl.loop(0, SECTION_A // GROUP)
         def _(step):
-            rows = rows_at(step, GROUP * SECTION_B)
             for i in range(2):
                 at = (2 * part + i) * LANES
-                restored[rows, at : at + LANES] = by_j[i, rows, :].astype(jnp.bfloat16)
+                for g in range(GROUP):
+                    rows = rows_at(step * GROUP + g, SECTION_B)
+                    restored[rows, at : at + LANES] = by_j[i, padded(step, g, SECTION_B), :].astype(
+                        jnp.bfloat16
+                    )
 
     @pl.loop(0, SECTION_A // GROUP)
     def _(step):
@@ -276,8 +286,8 @@
         in_specs=[whole] * (3 + len(tables)),
         out_specs=(whole, whole),
         scratch_shapes=[
-            pltpu.VMEM((2, NCH, LANES), jnp.float32),
-            pltpu.VMEM((2, NCH, LANES), jnp.float32),
+            pltpu.VMEM((2, SECTION_B * PITCH_Q, LANES), jnp.float32),
+            pltpu.VMEM((2, SECTION_A * PITCH_J, LANES), jnp.float32),
             pltpu.VMEM((NCH, 2 * BINS), jnp.bfloat16),
         ],
         compiler_params=pltpu.CompilerParams(vmem_limit_bytes=60 * 1024 * 1024),

time: 467 us -> 407 us (0.87)
  Pallas kernels: 109 us -> 49.4 us
    pallas_call x1, Pallas kernels: 109 us -> 49.4 us  [filter_frame(): pl.pallas_call(frame_kernel, out_shape=(half, half), in_specs=[whole] * (...]
  transfers between devices with their start and end apart: 4 -> 4, of which waited for: 3 -> 3; matrix products, arithmetic and copies ran while one was open for 4% -> 5% of each run, Pallas kernels for 0% -> 0%
where the time goes in v2:
time: 407 us; the launch traced here: 406 us
  waiting for transfers between devices  191 us (47%)
  blocking collectives  102 us (25%)
  Pallas kernels  49.4 us (12%)
  local copies, waits for them, and re-layouts  25.5 us (6%)
  other arithmetic  13.9 us (3%)
  between operations  13.6 us (3%)
  starting transfers between devices  10.7 us (3%)
    all_to_all x1, waiting for transfers between devices, frames_body(): lax.all_to_all(record, 'chan', split_axis=1, concat_axis=0, tiled=True)  116 us
    all_to_all x1, blocking collectives, frames_body(): lax.all_to_all(result, 'chan', split_axis=0, concat_axis=1, tiled=True)  102 us
    ppermute x2, waiting for transfers between devices, shifted(): return lax.ppermute(value, axes, pairs)  75.4 us
    pallas_call x1, Pallas kernels, filter_frame(): pl.pallas_call(frame_kernel, out_shape=(half, half), in_specs=[whole] * (...  49.4 us
  transfers between devices with their start and end apart: 4, of which 3 were waited for; matrix products, arithmetic and copies ran while one was open for 5% of the time, Pallas kernels for 0%

profile of v2, /device:TPU:15, one launch (start us, length us, event | category | flops | bytes accessed | tf_op | source)
XLA Modules:
  0.0 406.1 jit_solution(10114325531659185905)
XLA Ops:
  6.5 4.6 %copy.52 = bf16[64,16,8,256]{3,2,0,1:T(8,128)(2,1)} copy(bf16[64,16,8,256]{3,2,1,0:T(8,128)(2,1)} %bitcast.63) | data formatting | bytes 8388608 | tf_op jit(solution)/shard_map/all_to_all | solution.py:314
  11.2 6.7 %all-to-all-start = ((bf16[512,16,256]{2,0,1:T(8,128)(2,1)}), bf16[512,16,256]{2,0,1:T(8,128)(2,1)}, u32[]{:S(2)}, u32[]{:S(2)}) async-start(bf16[512,16,256]{2,0,1:T(8,128)(2,1)} %bitcast.62), calls=%async_computation | async-start | bytes 8388608 | tf_op jit(solution)/shard_map/all_to_all | solution.py:314
  17.9 0.5 reshape.464
  18.5 0.2 copy.38
  18.7 0.9 copy.53
  19.6 116.0 %all-to-all-done = bf16[512,16,256]{2,0,1:T(8,128)(2,1)} async-done(((bf16[512,16,256]{2,0,1:T(8,128)(2,1)}), bf16[512,16,256]{2,0,1:T(8,128)(2,1)}, u32[]{:S(2)}, u32[]{:S(2)}) %all-to-all-start) | async-done | bytes 4194336 | tf_op jit(solution)/shard_map/all_to_all | solution.py:314
  135.6 2.1 collective-permute-start
  138.6 0.7 reshape.460.w_one
  139.5 0.7 reshape.463.w_four
  140.2 0.3 fusion.33
  140.5 0.3 multiply_convert_fusion.2
  140.8 0.3 cosine_convert_fusion.1
  141.0 0.3 negate_convert_fusion.2
  141.3 0.3 negate_convert_fusion.1
  141.8 0.7 copy.55
  142.6 0.7 copy.54
  143.3 0.7 multiply_subtract_fusion.taper
  143.9 2.5 multiply_convert_fusion.1
  146.4 0.9 pad_maximum_fusion
  147.3 2.2 cosine_convert_fusion
  149.5 0.9 copy_bitcast_fusion.1.fwd_time
  150.6 6.4 %copy.39 = bf16[256,8192]{0,1:T(8,128)(2,1)} copy(bf16[256,8192]{1,0:T(8,128)(2,1)} %all-gather.2.cloned.1.call-done) | data formatting | bytes 8388608 | tf_op jit(solution)/shard_map/all_gather | solution.py:312
  157.0 29.6 %collective-permute-done.second = bf16[8192,256]{1,0:T(8,128)(2,1)} collective-permute-done((bf16[8192,256]{1,0:T(8,128)(2,1)}, bf16[8192,256]{1,0:T(8,128)(2,1)}, u32[]{:S(2)}, u32[]{:S(2)}) %collective-permute-start) | collective-permute-done | bytes 4194336 | tf_op jit(solution)/shard_map/ppermute | solution.py:304
  186.6 2.5 broadcast_in_dim.15.tw_sin
  189.2 2.6 broadcast_in_dim.14.tw_cos
  191.8 49.4 %shard_map.28 = (bf16[8192,256]{1,0:T(8,128)(2,1)}, bf16[8192,256]{1,0:T(8,128)(2,1)}) custom-call(bf16[8192,256]{1,0:T(8,128)(2,1)} %bitcast.1.first, bf16[8192,256]{1,0:T(8,128)(2,1)} %collective-permute-done.second, f32[1,512]{1,0:T(1,128)} %multiply_subtract_fusion.taper, bf16[2,512,256]{2,1,0:T(8,128)(2,1)} %copy_bitcast_fusion.1.fwd_time, ...), custom_call_target="tpu_custom_call" | custom-call | flops 16000000000 | bytes 30000000 | tf_op jit(solution)/shard_map/pallas_call | solution.py:283
  241.2 1.9 collective-permute-start.1
  243.1 45.7 %collective-permute-done.1 = bf16[8192,256]{1,0:T(8,128)(2,1)S(1)} collective-permute-done((bf16[8192,256]{1,0:T(8,128)(2,1)}, bf16[8192,256]{1,0:T(8,128)(2,1)S(1)}, u32[]{:S(2)}, u32[]{:S(2)}) %collective-permute-start.1) | collective-permute-done | bytes 4194336 | tf_op jit(solution)/shard_map/ppermute | solution.py:304
  288.9 3.5 add_convert_fusion
  292.4 101.6 %all_to_all.32 = bf16[16,512,256]{2,1,0:T(8,128)(2,1)S(1)} all-to-all(bf16[16,512,256]{2,1,0:T(8,128)(2,1)S(1)} %bitcast.61), channel_id=1, replica_groups=mesh['tm'=2,'chan'=16] {'chan'}, dimensions={0} | all-to-all | bytes 8388608 | tf_op jit(solution)/shard_map/all_to_all | solution.py:326
  394.0 0.9 convert_bitcast_fusion
  394.9 4.4 %copy.43 = f32[16,64,8,256]{3,2,0,1:T(8,128)} copy(f32[16,64,8,256]{3,2,1,0:T(8,128)S(1)} %convert_bitcast_fusion) | data formatting | bytes 16777216 | tf_op jit(solution)/shard_map/convert_element_type | solution.py:327
  (24 shorter events, 1.6 us)
Async XLA Ops:
  11.2 6.7 %copy-start = (s32[16,8192]{1,0:T(8,128)S(1)}, s32[16,8192]{1,0:T(8,128)}, u32[]{:S(2)}) copy-start(s32[16,8192]{1,0:T(8,128)} %param.3) | copy-start | bytes 1572868
  11.2 124.4 %all-to-all-start = ((bf16[512,16,256]{2,0,1:T(8,128)(2,1)}), bf16[512,16,256]{2,0,1:T(8,128)(2,1)}, u32[]{:S(2)}, u32[]{:S(2)}) async-start(bf16[512,16,256]{2,0,1:T(8,128)(2,1)} %bitcast.62), calls=%async_computation | async-start | bytes 8388608 | tf_op jit(solution)/shard_map/all_to_all | solution.py:314
  17.8 132.7 %all-gather.2.cloned.1.call-start = ((), (), s32[]{:S(2)}) async-start(), calls=%async_computation.2 | async-start | bytes 4456448 | tf_op jit(solution)/shard_map/all_gather | solution.py:312
  135.6 51.0 %collective-permute-start = (bf16[8192,256]{1,0:T(8,128)(2,1)}, bf16[8192,256]{1,0:T(8,128)(2,1)}, u32[]{:S(2)}, u32[]{:S(2)}) collective-permute-start(bf16[8192,256]{1,0:T(8,128)(2,1)} %bitcast.1.first), channel_id=1, source_target_pairs={{1,0},{2,1},{3,2},{4,3},{5,4},{6,5},{7,6},{8,7},{9,8},{10,9},{11,1... | collective-permute-start | bytes 12582920 | tf_op jit(solution)/shard_map/ppermute | solution.py:304
  241.2 47.7 %collective-permute-start.1 = (bf16[8192,256]{1,0:T(8,128)(2,1)}, bf16[8192,256]{1,0:T(8,128)(2,1)S(1)}, u32[]{:S(2)}, u32[]{:S(2)}) collective-permute-start(bf16[8192,256]{1,0:T(8,128)(2,1)} %get-tuple-element.8), channel_id=1, source_target_pairs={{0,1},{1,2},{2,3},{3,4},{4,5},{5,6},{6,7},{7,8},{8,9},{9,10},{10,1... | collective-permute-start | bytes 12582920 | tf_op jit(solution)/shard_map/ppermute | solution.py:304
Sparse Core Ops, SparseCore 0:
  20.8 94.8 all-gather.1

commit v3 on v2

--- a/solution.py
+++ b/solution.py
@@ -297,11 +297,260 @@
     )(first, second, *tables, gate)
 
 
-def shifted(value, by):
-    axes = ("tm", "chan")
-    peers = lax.axis_size("tm") * lax.axis_size("chan")
-    pairs = [(i, i + by) for i in range(peers) if 0 <= i + by < peers]
-    return lax.ppermute(value, axes, pairs)
+def device_at(group, place):
+    peers = lax.axis_size("chan")
+    place = place + (group % 2) * (peers - 1 - 2 * place)
+    if peers % 4 == 0:
+        place = place + (place // 4 % 2) * (2 - 4 * (place // 2 % 2))
+    return place
+
+
+def place_of(group, device):
+    peers = lax.axis_size("chan")
+    if peers % 4 == 0:
+        device = device + (device // 4 % 2) * (2 - 4 * (device // 2 % 2))
+    return device + (group % 2) * (peers - 1 - 2 * device)
+
+
+def along_line(group, place, by):
+    peers = lax.axis_size("chan")
+    spot = group * peers + place + by
+    there = spot // peers
+    return {"tm": there, "chan": device_at(there, spot % peers)}
+
+
+def greet(group, me, place):
+    groups, peers = lax.axis_size("tm"), lax.axis_size("chan")
+    barrier = pltpu.get_barrier_semaphore()
+
+    def signal(target):
+        pl.semaphore_signal(barrier, inc=1, device_id=target, device_id_type=pl.DeviceIdType.MESH)
+
+    @pl.loop(1, peers)
+    def _(i):
+        signal({"tm": group, "chan": lax.rem(me + i, peers)})
+
+    up = jnp.logical_and(place == 0, group > 0)
+    down = jnp.logical_and(place == peers - 1, group < groups - 1)
+
+    @pl.when(up)
+    def _():
+        signal(along_line(group, place, -1))
+
+    @pl.when(down)
+    def _():
+        signal(along_line(group, place, 1))
+
+    pl.semaphore_wait(barrier, peers - 1 + up.astype(jnp.int32) + down.astype(jnp.int32))
+
+
+def remote(source, target, send_sem, recv_sem, device):
+    return pltpu.make_async_remote_copy(
+        src_ref=source,
+        dst_ref=target,
+        send_sem=send_sem,
+        recv_sem=recv_sem,
+        device_id=device,
+        device_id_type=pl.DeviceIdType.MESH,
+    )
+
+
+def gather_kernel(record, first, second, nothing, send, recv, pass_send, pass_recv, local):
+    groups, peers = lax.axis_size("tm"), lax.axis_size("chan")
+    group, me = lax.axis_index("tm"), lax.axis_index("chan")
+    place = place_of(group, me)
+    size = record.shape[0]
+    has_prev = jnp.logical_or(place > 0, group > 0)
+    has_next = jnp.logical_or(place < peers - 1, group < groups - 1)
+
+    def rows(device):
+        return pl.ds(pl.multiple_of(device * size, size), size)
+
+    def block(device):
+        return record.at[:, pl.ds(pl.multiple_of(place_of(group, device) * HOP, HOP), HOP)]
+
+    def sent(device):
+        return remote(
+            block(device), first.at[rows(me)], send.at[device], recv.at[me],
+            {"tm": group, "chan": device},
+        )
+
+    def arriving(device):
+        return remote(
+            block(device), first.at[rows(device)], send.at[device], recv.at[device],
+            {"tm": group, "chan": device},
+        )
+
+    def passed(source, device):
+        return remote(
+            source, second.at[rows(device)], pass_send.at[device], pass_recv.at[device],
+            along_line(group, place, -1),
+        )
+
+    greet(group, me, place)
+    own = pltpu.make_async_copy(block(me), first.at[rows(me)], local)
+    own.start()
+
+    @pl.loop(1, peers)
+    def _(i):
+        sent(lax.rem(me + i, peers)).start()
+
+    @pl.when(has_prev)
+    def _():
+        passed(block(me), me).start()
+
+    @pl.loop(1, peers)
+    def _(i):
+        device = lax.rem(me + peers - i, peers)
+        arriving(device).wait_recv()
+
+        @pl.when(has_prev)
+        def _():
+            passed(first.at[rows(device)], device).start()
+
+    own.wait()
+
+    @pl.loop(1, peers)
+    def _(i):
+        sent(lax.rem(me + i, peers)).wait_send()
+
+    @pl.when(has_prev)
+    def _():
+        @pl.loop(0, peers)
+        def _(i):
+            passed(first.at[rows(i)], i).wait_send()
+
+    @pl.when(has_next)
+    def _():
+        @pl.loop(0, peers)
+        def _(i):
+            passed(first.at[rows(i)], i).wait_recv()
+
+    @pl.when(jnp.logical_not(has_next))
+    def _():
+        nothing[...] = jnp.zeros_like(nothing)
+
+        @pl.loop(0, peers)
+        def _(i):
+            fill = pltpu.make_async_copy(nothing, second.at[rows(i)], local)
+            fill.start()
+            fill.wait()
+
+
+def scatter_kernel(head, tail, out, carried, total, send, recv, pass_send, pass_recv, local):
+    groups, peers = lax.axis_size("tm"), lax.axis_size("chan")
+    group, me = lax.axis_index("tm"), lax.axis_index("chan")
+    place = place_of(group, me)
+    size = out.shape[0]
+    has_prev = jnp.logical_or(place > 0, group > 0)
+    has_next = jnp.logical_or(place < peers - 1, group < groups - 1)
+    after = along_line(group, place, 1)
+
+    def rows(device):
+        return pl.ds(pl.multiple_of(device * size, size), size)
+
+    def block(device):
+        return out.at[:, pl.ds(pl.multiple_of(place_of(group, device) * HOP, HOP), HOP)]
+
+    def passed(device):
+        return remote(
+            tail.at[rows(device)], carried.at[rows(device)], pass_send.at[device],
+            pass_recv.at[device], after,
+        )
+
+    def sent(device):
+        return remote(
+            total.at[rows(device)], block(me), send.at[device], recv.at[me],
+            {"tm": group, "chan": device},
+        )
+
+    def arriving(device):
+        return remote(
+            total.at[rows(device)], block(device), send.at[device], recv.at[device],
+            {"tm": group, "chan": device},
+        )
+
+    def add(device):
+        @pl.when(has_prev)
+        def _():
+            passed(device).wait_recv()
+            total[rows(device), :] = (
+                head[rows(device), :].astype(jnp.float32)
+                + carried[rows(device), :].astype(jnp.float32)
+            ).astype(total.dtype)
+
+        @pl.when(jnp.logical_not(has_prev))
+        def _():
+            total[rows(device), :] = head[rows(device), :]
+
+    greet(group, me, place)
+
+    @pl.when(has_next)
+    def _():
+        @pl.loop(1, peers + 1)
+        def _(i):
+            passed(lax.rem(after["chan"] + i, peers)).start()
+
+    @pl.loop(1, peers)
+    def _(i):
+        device = lax.rem(me + i, peers)
+        add(device)
+        sent(device).start()
+
+    add(me)
+    own = pltpu.make_async_copy(total.at[rows(me)], block(me), local)
+    own.start()
+    own.wait()
+
+    @pl.loop(1, peers)
+    def _(i):
+        arriving(lax.rem(me + peers - i, peers)).wait_recv()
+
+    @pl.loop(1, peers)
+    def _(i):
+        sent(lax.rem(me + i, peers)).wait_send()
+
+    @pl.when(has_next)
+    def _():
+        @pl.loop(0, peers)
+        def _(i):
+            passed(i).wait_send()
+
+
+def exchange_scratch():
+    peers = lax.axis_size("chan")
+    return [pltpu.SemaphoreType.DMA((peers,))] * 4 + [pltpu.SemaphoreType.DMA]
+
+
+def gather_frames(record):
+    anywhere = pl.BlockSpec(memory_space=pl.ANY)
+    half = jax.ShapeDtypeStruct((NCH, HOP), record.dtype)
+    return pl.pallas_call(
+        gather_kernel,
+        out_shape=(half, half),
+        in_specs=[anywhere],
+        out_specs=(anywhere, anywhere),
+        scratch_shapes=[pltpu.VMEM((record.shape[0], HOP), record.dtype)] + exchange_scratch(),
+        compiler_params=pltpu.CompilerParams(
+            collective_id=0, has_side_effects=True, vmem_limit_bytes=60 * 1024 * 1024
+        ),
+        cost_estimate=pl.CostEstimate(flops=0, bytes_accessed=300_000_000, transcendentals=0),
+    )(record)
+
+
+def scatter_frames(head, tail, channels, span_len):
+    anywhere = pl.BlockSpec(memory_space=pl.ANY)
+    return pl.pallas_call(
+        scatter_kernel,
+        out_shape=jax.ShapeDtypeStruct((channels, span_len), head.dtype),
+        in_specs=[pl.BlockSpec(memory_space=pltpu.VMEM), anywhere],
+        out_specs=anywhere,
+        scratch_shapes=[pltpu.VMEM((NCH, HOP), head.dtype)] * 2 + exchange_scratch(),
+        compiler_params=pltpu.CompilerParams(
+            collective_id=1, has_side_effects=True, vmem_limit_bytes=60 * 1024 * 1024
+        ),
+        cost_estimate=pl.CostEstimate(flops=0, bytes_accessed=300_000_000, transcendentals=0),
+    )(head, tail)
 
 
 def frames_body(record, fan_mask):
@@ -310,25 +559,13 @@
     gate = fan_mask.astype(jnp.bfloat16).reshape(local_bins, SECTION_B, SECTION_A)
     gate = gate.transpose(0, 2, 1).reshape(local_bins, NCH)
     gate = lax.all_gather(gate, "chan", axis=0, tiled=True).T
-    tables = frame_tables()
-    mine = lax.all_to_all(record, "chan", split_axis=1, concat_axis=0, tiled=True)
-    after = shifted(mine[:, :HOP], -1)
-    held = mine.shape[1] // HOP
-    blocks = [mine[:, f * HOP : (f + 1) * HOP] for f in range(held)] + [after]
-    halves = [filter_frame(blocks[f], blocks[f + 1], tables, gate) for f in range(held)]
-    before = shifted(halves[-1][1], 1)
-    tails = [before] + [halves[f][1] for f in range(held - 1)]
-    sums = [
-        (halves[f][0].astype(jnp.float32) + tails[f].astype(jnp.float32)).astype(jnp.bfloat16)
-        for f in range(held)
-    ]
-    result = sums[0] if held == 1 else jnp.concatenate(sums, axis=1)
-    result = lax.all_to_all(result, "chan", split_axis=0, concat_axis=1, tiled=True)
-    return result.astype(jnp.float32)
+    first, second = gather_frames(record)
+    head, tail = filter_frame(first, second, frame_tables(), gate)
+    return scatter_frames(head, tail, channels, span_len).astype(jnp.float32)
 
 
 def body(record, fan_mask):
-    if (record.shape[1] // HOP) % lax.axis_size("chan") == 0:
+    if record.shape[1] // HOP == lax.axis_size("chan"):
         return frames_body(record, fan_mask)
     return bins_body(record, fan_mask)
 

time: 407 us -> 404 us (level)
  Pallas kernels: 49.4 us -> 357 us
  waiting for transfers between devices: 191 us -> 0.04 us
  blocking collectives: 102 us -> 0 us
  starting transfers between devices: 10.7 us -> 0.01 us
  local copies, waits for them, and re-layouts: 25.5 us -> 16.5 us
    pallas_call x0 -> x2, Pallas kernels: none -> 307 us  [the longest x1 175 us: scatter_frames(): pl.pallas_call(scatter_kernel, out_shape=jax.ShapeDtypeStruct((channels,...]
    all_to_all x1 -> x0, waiting for transfers between devices: 116 us -> none  [frames_body(): lax.all_to_all(record, 'chan', split_axis=1, concat_axis=0, tiled=True)]
    all_to_all x1 -> x0, blocking collectives: 102 us -> none  [frames_body(): lax.all_to_all(result, 'chan', split_axis=0, concat_axis=1, tiled=True)]
    ppermute x2 -> x0, waiting for transfers between devices: 75.4 us -> none  [shifted(): return lax.ppermute(value, axes, pairs)]
    all_to_all x1 -> x0, starting transfers between devices: 6.69 us -> none  [frames_body(): lax.all_to_all(record, 'chan', split_axis=1, concat_axis=0, tiled=True)]
    all_to_all x1 -> x0, local copies, waits for them, and re-layouts: 4.62 us -> none  [frames_body(): lax.all_to_all(record, 'chan', split_axis=1, concat_axis=0, tiled=True)]
    convert_element_type x1 -> x0, local copies, waits for them, and re-layouts: 4.41 us -> none  [frames_body(): return result.astype(jnp.float32)]
  transfers between devices with their start and end apart: 4 -> 1, of which waited for: 3 -> 0; matrix products, arithmetic and copies ran while one was open for 5% -> 3% of each run, Pallas kernels for 0% -> 33%
where the time goes in v3:
time: 404 us
  Pallas kernels  357 us (88%)
  other arithmetic  17.1 us (4%)
  local copies, waits for them, and re-layouts  16.5 us (4%)
  between operations  13.6 us (3%)
    pallas_call x1, Pallas kernels, scatter_frames(): pl.pallas_call(scatter_kernel, out_shape=jax.ShapeDtypeStruct((channels,...  175 us
    pallas_call x1, Pallas kernels, gather_frames(): pl.pallas_call(gather_kernel, out_shape=(half, half), in_specs=[anywhere]...  132 us
    pallas_call x1, Pallas kernels, filter_frame(): pl.pallas_call(frame_kernel, out_shape=(half, half), in_specs=[whole] * (...  49.4 us
  transfers between devices with their start and end apart: 1, of which 0 were waited for; matrix products, arithmetic and copies ran while one was open for 3% of the time, Pallas kernels for 33%

profile of v3, /device:TPU:15, one launch (start us, length us, event | category | flops | bytes accessed | tf_op | source)
XLA Modules:
  0.0 403.8 jit_solution(10408905426920834075)
XLA Ops:
  6.5 1.1 convert_element_type.155
  7.6 0.5 reshape.456
  8.2 0.2 copy.29
  8.4 0.9 copy.39
  9.3 0.1 fusion.38
  9.4 0.1 multiply_convert_fusion.3
  9.6 0.1 cosine_convert_fusion.2
  9.7 0.1 negate_convert_fusion.4
  9.9 0.1 negate_convert_fusion.3
  10.2 0.7 reshape.452.w_one
  11.0 0.7 reshape.455.w_four
  11.8 0.3 fusion.33
  12.1 0.3 multiply_convert_fusion.2
  12.4 0.3 cosine_convert_fusion.1
  12.6 0.3 negate_convert_fusion.2
  12.9 0.3 negate_convert_fusion.1
  13.2 0.1 copy.26
  13.4 0.7 copy.41
  14.2 0.7 copy.40
  14.8 132.3 %shard_map.28 = (bf16[8192,256]{1,0:T(8,128)(2,1)}, bf16[8192,256]{1,0:T(8,128)(2,1)}) custom-call(bf16[512,4096]{1,0:T(8,128)(2,1)} %record.1), custom_call_target="tpu_custom_call" | custom-call | bytes 300000000 | tf_op jit(solution)/shard_map/pallas_call | solution.py:528
  147.2 0.6 multiply_subtract_fusion.taper
  147.8 2.5 multiply_convert_fusion.1
  150.3 0.9 pad_maximum_fusion
  151.2 2.2 cosine_convert_fusion
  153.4 0.9 copy_bitcast_fusion.fwd_time
  154.3 0.1 fusion.39
  154.5 6.4 %copy.30 = bf16[256,8192]{0,1:T(8,128)(2,1)} copy(bf16[256,8192]{1,0:T(8,128)(2,1)} %all-gather.2.cloned.1.call-done) | data formatting | bytes 8388608 | tf_op jit(solution)/shard_map/all_gather | solution.py:561
  160.9 2.6 broadcast_in_dim.15.tw_sin
  163.4 2.6 broadcast_in_dim.14.tw_cos
  166.0 49.4 %shard_map.29 = (bf16[8192,256]{1,0:T(8,128)(2,1)}, bf16[8192,256]{1,0:T(8,128)(2,1)}) custom-call(bf16[8192,256]{1,0:T(8,128)(2,1)} %get-tuple-element.9.first, bf16[8192,256]{1,0:T(8,128)(2,1)} %get-tuple-element.10.second, f32[1,512]{1,0:T(1,128)} %multiply_subtract_fusion.taper, bf16[2,512,256]{2,1,0:T(8,128)(2,1)} %copy_bitcast_fusion.fwd_time, ...), custom_call_target="tpu_custom_call" | custom-call | flops 16000000000 | bytes 30000000 | tf_op jit(solution)/shard_map/pallas_call | solution.py:283
  215.4 174.9 %shard_map.30 = bf16[512,4096]{1,0:T(8,128)(2,1)} custom-call(bf16[8192,256]{1,0:T(8,128)(2,1)} %get-tuple-element.11.head, bf16[8192,256]{1,0:T(8,128)(2,1)} %get-tuple-element.12.tail), custom_call_target="tpu_custom_call" | custom-call | bytes 300000000 | tf_op jit(solution)/shard_map/pallas_call | solution.py:543
  390.3 6.7 %convert_element_type.156 = f32[512,4096]{1,0:T(8,128)} convert(bf16[512,4096]{1,0:T(8,128)(2,1)} %shard_map.30) | non-fusion elementwise | flops 2097152 | bytes 12582912 | tf_op jit(solution)/shard_map/convert_element_type | solution.py:564
  (14 shorter events, 0.6 us)
Async XLA Ops:
  6.5 147.9 %all-gather.2.cloned.1.call-start = ((), (), s32[]{:S(2)}) async-start(), calls=%async_computation | async-start | bytes 4456448 | tf_op jit(solution)/shard_map/all_gather | solution.py:561
Sparse Core Ops, SparseCore 0:
  9.5 131.6 all-gather.1

commit v4 on v3

--- a/solution.py
+++ b/solution.py
@@ -1,8 +1,8 @@
-import functools
 import math
 
 import jax
 import jax.numpy as jnp
+import numpy as np
 from jax import lax
 from jax.experimental import pallas as pl
 from jax.experimental.pallas import tpu as pltpu
@@ -23,41 +23,41 @@
 
 
 def hann_taper(length):
-    steps = jnp.arange(length, dtype=jnp.int32).astype(jnp.float32)
-    return 0.5 - 0.5 * jnp.cos(steps * (2.0 * math.pi / length))
+    steps = np.arange(length, dtype=jnp.int32).astype(jnp.float32)
+    return 0.5 - 0.5 * np.cos(steps * (2.0 * math.pi / length))
 
 
 def time_table(length, bins):
-    rows = jnp.arange(length, dtype=jnp.int32)[:, None]
-    cols = jnp.arange(bins, dtype=jnp.int32)[None, :]
+    rows = np.arange(length, dtype=jnp.int32)[:, None]
+    cols = np.arange(bins, dtype=jnp.int32)[None, :]
     phase = (rows * cols % length).astype(jnp.float32) * (2.0 * math.pi / length)
-    return jnp.concatenate([jnp.cos(phase), -jnp.sin(phase)], axis=1).astype(jnp.bfloat16)
+    return np.concatenate([np.cos(phase), -np.sin(phase)], axis=1).astype(jnp.bfloat16)
 
 
 def inverse_time_table(length, bins):
-    rows = jnp.arange(bins, dtype=jnp.int32)[:, None]
-    cols = jnp.arange(length, dtype=jnp.int32)[None, :]
+    rows = np.arange(bins, dtype=jnp.int32)[:, None]
+    cols = np.arange(length, dtype=jnp.int32)[None, :]
     phase = (rows * cols % length).astype(jnp.float32) * (2.0 * math.pi / length)
-    weight = jnp.where(rows == 0, 1.0, 2.0).astype(jnp.float32) / length
-    return jnp.stack([weight * jnp.cos(phase), -weight * jnp.sin(phase)]).astype(jnp.bfloat16)
+    weight = np.where(rows == 0, 1.0, 2.0).astype(jnp.float32) / length
+    return np.stack([weight * np.cos(phase), -weight * np.sin(phase)]).astype(jnp.bfloat16)
 
 
 def block_table(order_len, exponent_sign):
-    rows = jnp.arange(order_len, dtype=jnp.int32)[:, None]
-    cols = jnp.arange(order_len, dtype=jnp.int32)[None, :]
+    rows = np.arange(order_len, dtype=jnp.int32)[:, None]
+    cols = np.arange(order_len, dtype=jnp.int32)[None, :]
     phase = (rows * cols % order_len).astype(jnp.float32) * (2.0 * math.pi / order_len)
-    cosine = jnp.cos(phase)
-    sine = exponent_sign * jnp.sin(phase)
-    real_row = jnp.stack([cosine, sine], axis=1)
-    imag_row = jnp.stack([-sine, cosine], axis=1)
-    return jnp.stack([real_row, imag_row], axis=0).astype(jnp.bfloat16)
+    cosine = np.cos(phase)
+    sine = exponent_sign * np.sin(phase)
+    real_row = np.stack([cosine, sine], axis=1)
+    imag_row = np.stack([-sine, cosine], axis=1)
+    return np.stack([real_row, imag_row], axis=0).astype(jnp.bfloat16)
 
 
 def twiddle_pair(row_count, col_count, total, exponent_sign):
-    rows = jnp.arange(row_count, dtype=jnp.int32)[:, None]
-    cols = jnp.arange(col_count, dtype=jnp.int32)[None, :]
+    rows = np.arange(row_count, dtype=jnp.int32)[:, None]
+    cols = np.arange(col_count, dtype=jnp.int32)[None, :]
     phase = (rows * cols % total).astype(jnp.float32) * (2.0 * math.pi / total)
-    return (jnp.cos(phase), exponent_sign * jnp.sin(phase))
+    return (np.cos(phase), exponent_sign * np.sin(phase))
 
 
 def rotate(values, cosine, sine):
@@ -199,7 +199,7 @@
                 columns.append(
                     jnp.concatenate([by_j[0, held, :], by_j[1, held, :]], axis=0).astype(jnp.bfloat16)
                 )
-                gates.append(gate[rows, lanes].astype(jnp.float32))
+                gates.append(gate[lanes, rows].astype(jnp.float32).T)
             plane = jnp.dot(
                 w_two[...], jnp.concatenate(columns, axis=1), preferred_element_type=jnp.float32
             )
@@ -272,8 +272,8 @@
         flat_table(SECTION_B, -1.0),
         flat_table(SECTION_B, 1.0),
         flat_table(SECTION_A, 1.0),
-        jnp.broadcast_to(tw_cos[:, :, None], spread).reshape(NCH, LANES),
-        jnp.broadcast_to(tw_sin[:, :, None], spread).reshape(NCH, LANES),
+        np.broadcast_to(tw_cos[:, :, None], spread).reshape(NCH, LANES),
+        np.broadcast_to(tw_sin[:, :, None], spread).reshape(NCH, LANES),
     )
 
 
@@ -319,6 +319,13 @@
     return {"tm": there, "chan": device_at(there, spot % peers)}
 
 
+def offset_of(step):
+    peers = lax.axis_size("chan")
+    if peers % 2 == 1:
+        return step + 1
+    return peers // 2 + (1 - 2 * (step % 2)) * ((step + 1) // 2)
+
+
 def greet(group, me, place):
     groups, peers = lax.axis_size("tm"), lax.axis_size("chan")
     barrier = pltpu.get_barrier_semaphore()
@@ -355,7 +362,15 @@
     )
 
 
-def gather_kernel(record, first, second, nothing, send, recv, pass_send, pass_recv, local):
+EDGE = 4
+
+
+def edge_places():
+    peers = lax.axis_size("chan")
+    return list(range(EDGE, peers, EDGE)) if peers % EDGE == 0 else []
+
+
+def gather_kernel(record, first, second, nothing, send, recv, pass_send, pass_recv, local, edge_send):
     groups, peers = lax.axis_size("tm"), lax.axis_size("chan")
     group, me = lax.axis_index("tm"), lax.axis_index("chan")
     place = place_of(group, me)
@@ -363,11 +378,25 @@
     has_prev = jnp.logical_or(place > 0, group > 0)
     has_next = jnp.logical_or(place < peers - 1, group < groups - 1)
 
+    edges = edge_places()
+    starts = jnp.logical_and(place > 0, place % EDGE == 0) if edges else place < 0
+    ends = jnp.logical_and(place < peers - 1, place % EDGE == EDGE - 1) if edges else place < 0
+    passes = jnp.logical_and(has_prev, jnp.logical_not(starts))
+
     def rows(device):
         return pl.ds(pl.multiple_of(device * size, size), size)
 
+    def block_at(spot):
+        return record.at[:, pl.ds(pl.multiple_of(spot * HOP, HOP), HOP)]
+
     def block(device):
-        return record.at[:, pl.ds(pl.multiple_of(place_of(group, device) * HOP, HOP), HOP)]
+        return block_at(place_of(group, device))
+
+    def edged(at, edge, device):
+        return remote(
+            block_at(edge), second.at[rows(me)], edge_send.at[at], pass_recv.at[me],
+            {"tm": group, "chan": device},
+        )
 
     def sent(device):
         return remote(
@@ -391,20 +420,31 @@
     own = pltpu.make_async_copy(block(me), first.at[rows(me)], local)
     own.start()
 
-    @pl.loop(1, peers)
+    @pl.loop(0, peers - 1)
     def _(i):
-        sent(lax.rem(me + i, peers)).start()
-
-    @pl.when(has_prev)
+        sent(lax.rem(me + offset_of(i), peers)).start()
+
+    for at, edge in enumerate(edges):
+        to = device_at(group, edge - 1)
+
+        @pl.when(to != me)
+        def _():
+            edged(at, edge, to).start()
+
+        @pl.when(to == me)
+        def _():
+            pltpu.make_async_copy(block_at(edge), second.at[rows(me)], edge_send.at[at]).start()
+
+    @pl.when(passes)
     def _():
         passed(block(me), me).start()
 
-    @pl.loop(1, peers)
+    @pl.loop(0, peers - 1)
     def _(i):
-        device = lax.rem(me + peers - i, peers)
+        device = lax.rem(me + peers - offset_of(i), peers)
         arriving(device).wait_recv()
 
-        @pl.when(has_prev)
+        @pl.when(passes)
         def _():
             passed(first.at[rows(device)], device).start()
 
@@ -414,17 +454,33 @@
     def _(i):
         sent(lax.rem(me + i, peers)).wait_send()
 
-    @pl.when(has_prev)
+    @pl.when(passes)
     def _():
         @pl.loop(0, peers)
         def _(i):
             passed(first.at[rows(i)], i).wait_send()
 
+    for at, edge in enumerate(edges):
+        to = device_at(group, edge - 1)
+
+        @pl.when(to != me)
+        def _():
+            edged(at, edge, to).wait_send()
+
+        @pl.when(to == me)
+        def _():
+            pltpu.make_async_copy(block_at(edge), second.at[rows(me)], edge_send.at[at]).wait()
+
     @pl.when(has_next)
     def _():
-        @pl.loop(0, peers)
+        @pl.loop(1, peers)
         def _(i):
-            passed(first.at[rows(i)], i).wait_recv()
+            device = lax.rem(me + i, peers)
+            passed(first.at[rows(device)], device).wait_recv()
+
+    @pl.when(jnp.logical_and(has_next, jnp.logical_not(ends)))
+    def _():
+        passed(first.at[rows(me)], me).wait_recv()
 
     @pl.when(jnp.logical_not(has_next))
     def _():
@@ -487,13 +543,15 @@
 
     @pl.when(has_next)
     def _():
-        @pl.loop(1, peers + 1)
+        @pl.loop(0, peers - 1)
         def _(i):
-            passed(lax.rem(after["chan"] + i, peers)).start()
-
-    @pl.loop(1, peers)
+            passed(lax.rem(after["chan"] + offset_of(i), peers)).start()
+
+        passed(after["chan"]).start()
+
+    @pl.loop(0, peers - 1)
     def _(i):
-        device = lax.rem(me + i, peers)
+        device = lax.rem(me + offset_of(i), peers)
         add(device)
         sent(device).start()
 
@@ -530,7 +588,8 @@
         out_shape=(half, half),
         in_specs=[anywhere],
         out_specs=(anywhere, anywhere),
-        scratch_shapes=[pltpu.VMEM((record.shape[0], HOP), record.dtype)] + exchange_scratch(),
+        scratch_shapes=[pltpu.VMEM((record.shape[0], HOP), record.dtype)] + exchange_scratch()
+        + [pltpu.SemaphoreType.DMA((max(len(edge_places()), 1),))],
         compiler_params=pltpu.CompilerParams(
             collective_id=0, has_side_effects=True, vmem_limit_bytes=60 * 1024 * 1024
         ),
@@ -558,7 +617,7 @@
     local_bins = fan_mask.shape[0]
     gate = fan_mask.astype(jnp.bfloat16).reshape(local_bins, SECTION_B, SECTION_A)
     gate = gate.transpose(0, 2, 1).reshape(local_bins, NCH)
-    gate = lax.all_gather(gate, "chan", axis=0, tiled=True).T
+    gate = lax.all_gather(gate, "chan", axis=0, tiled=True)
     first, second = gather_frames(record)
     head, tail = filter_frame(first, second, frame_tables(), gate)
     return scatter_frames(head, tail, channels, span_len).astype(jnp.float32)

time: 404 us -> 377 us (0.933)
  Pallas kernels: 357 us -> 347 us
  local copies, waits for them, and re-layouts: 16.5 us -> 6.86 us
  other arithmetic: 17.1 us -> 7.75 us
    pallas_call x1, Pallas kernels: 175 us -> 151 us  [scatter_frames(): pl.pallas_call(scatter_kernel, out_shape=jax.ShapeDtypeStruct((channels,...]
    pallas_call x1, Pallas kernels: 132 us -> 146 us  [gather_frames(): pl.pallas_call(gather_kernel, out_shape=(half, half), in_specs=[anywhere]...]
    another operation x15 -> x0, other arithmetic: 7.66 us -> none
    all_gather x1 -> x0, local copies, waits for them, and re-layouts: 6.4 us -> none  [frames_body(): gate = lax.all_gather(gate, 'chan', axis=0, tiled=True).T]
    another operation x0 -> x2, local copies, waits for them, and re-layouts: none -> 5.21 us
    broadcast_in_dim x2 -> x0, local copies, waits for them, and re-layouts: 5.18 us -> none  [the longest x1 2.61 us: frame_tables(): jnp.broadcast_to(tw_cos[:, :, None], spread).reshape(NCH, LANES)]
  transfers between devices with their start and end apart: 1 -> 1, of which waited for: 0 -> 0; matrix products, arithmetic and copies ran while one was open for 3% -> 0% of each run, Pallas kernels for 33% -> 39%
where the time goes in v4:
time: 377 us; the launch traced here: 375 us
  Pallas kernels  347 us (92%)
  between operations  13.4 us (4%)
  other arithmetic  7.75 us (2%)
  local copies, waits for them, and re-layouts  6.86 us (2%)
    pallas_call x1, Pallas kernels, scatter_frames(): pl.pallas_call(scatter_kernel, out_shape=jax.ShapeDtypeStruct((channels,...  151 us
    pallas_call x1, Pallas kernels, gather_frames(): pl.pallas_call(gather_kernel, out_shape=(half, half), in_specs=[anywhere]...  146 us
    pallas_call x1, Pallas kernels, filter_frame(): pl.pallas_call(frame_kernel, out_shape=(half, half), in_specs=[whole] * (...  49.6 us
  transfers between devices with their start and end apart: 1, of which 0 were waited for; matrix products, arithmetic and copies ran while one was open for 0% of the time, Pallas kernels for 39%

profile of v4, /device:TPU:15, one launch (start us, length us, event | category | flops | bytes accessed | tf_op | source)
XLA Modules:
  0.0 375.4 jit_solution(10174925253235453170)
XLA Ops:
  6.5 0.0 copy-start.1
  6.5 0.0 all-gather.2.cloned.1.call-start
  6.5 1.1 convert_element_type.6
  7.6 0.5 reshape.6
  8.2 0.2 copy.13
  8.4 0.9 copy.16
  9.3 0.0 all-gather.2.cloned.1.call-update
  9.3 0.0 copy-start
  9.3 146.5 %shard_map.109 = (bf16[8192,256]{1,0:T(8,128)(2,1)}, bf16[8192,256]{1,0:T(8,128)(2,1)}) custom-call(bf16[512,4096]{1,0:T(8,128)(2,1)} %record.1), custom_call_target="tpu_custom_call" | custom-call | bytes 300000000 | tf_op jit(solution)/shard_map/pallas_call | solution.py:586
  155.8 0.0 all-gather.2.cloned.1.call-done.gate
  155.8 0.0 copy-done.1
  155.8 2.6 jit_solution_.6.tw_cos
  158.5 0.0 copy-done
  158.5 2.6 jit_solution_.7.tw_sin
  161.1 49.6 %shard_map.110 = (bf16[8192,256]{1,0:T(8,128)(2,1)}, bf16[8192,256]{1,0:T(8,128)(2,1)}) custom-call(bf16[8192,256]{1,0:T(8,128)(2,1)} %get-tuple-element.9.first, bf16[8192,256]{1,0:T(8,128)(2,1)} %get-tuple-element.10.second, f32[1,512]{1,0:T(1,128)} %constant.18.clone.taper, bf16[2,512,256]{2,1,0:T(8,128)(2,1)} %constant.19.clone.fwd_time, ...), custom_call_target="tpu_custom_call" | custom-call | flops 16000000000 | bytes 30000000 | tf_op jit(solution)/shard_map/pallas_call | solution.py:283
  210.7 151.2 %shard_map.111 = bf16[512,4096]{1,0:T(8,128)(2,1)} custom-call(bf16[8192,256]{1,0:T(8,128)(2,1)} %get-tuple-element.11.head, bf16[8192,256]{1,0:T(8,128)(2,1)} %get-tuple-element.12.tail), custom_call_target="tpu_custom_call" | custom-call | bytes 300000000 | tf_op jit(solution)/shard_map/pallas_call | solution.py:602
  361.9 6.7 %convert_element_type.7 = f32[512,4096]{1,0:T(8,128)} convert(bf16[512,4096]{1,0:T(8,128)(2,1)} %shard_map.111) | non-fusion elementwise | flops 2097152 | bytes 12582912 | tf_op jit(solution)/shard_map/convert_element_type | solution.py:623
Async XLA Ops:
  6.5 149.3 %copy-start.1 = (f32[8192]{0:T(1024)S(1)}, f32[8192]{0:T(1024)}, u32[]{:S(2)}) copy-start(f32[8192]{0:T(1024)} %constant.25.clone) | copy-start | bytes 98308
  6.5 149.3 %all-gather.2.cloned.1.call-start = ((), (), s32[]{:S(2)}) async-start(), calls=%async_computation | async-start | bytes 4456448 | tf_op jit(solution)/shard_map/all_gather | solution.py:620
  9.3 149.2 %copy-start = (f32[8192]{0:T(1024)S(1)}, f32[8192]{0:T(1024)}, u32[]{:S(2)}) copy-start(f32[8192]{0:T(1024)} %constant.26.clone) | copy-start | bytes 98308
Sparse Core Ops, SparseCore 0:
  9.5 110.5 all-gather.1

commit v5 on v4

--- a/solution.py
+++ b/solution.py
@@ -323,7 +323,8 @@
     peers = lax.axis_size("chan")
     if peers % 2 == 1:
         return step + 1
-    return peers // 2 + (1 - 2 * (step % 2)) * ((step + 1) // 2)
+    rank = step // 2 + (step % 2) * (peers // 2)
+    return peers // 2 + (1 - 2 * (rank % 2)) * ((rank + 1) // 2)
 
 
 def greet(group, me, place):
@@ -363,6 +364,8 @@
 
 
 EDGE = 4
+WINDOW = 5
+AHEAD = 3
 
 
 def edge_places():
@@ -420,39 +423,40 @@
     own = pltpu.make_async_copy(block(me), first.at[rows(me)], local)
     own.start()
 
-    @pl.loop(0, peers - 1)
+    @pl.when(passes)
+    def _():
+        passed(block(me), me).start()
+
+    @pl.loop(0, peers - 1 + WINDOW)
     def _(i):
-        sent(lax.rem(me + offset_of(i), peers)).start()
-
-    for at, edge in enumerate(edges):
-        to = device_at(group, edge - 1)
-
-        @pl.when(to != me)
-        def _():
-            edged(at, edge, to).start()
-
-        @pl.when(to == me)
-        def _():
-            pltpu.make_async_copy(block_at(edge), second.at[rows(me)], edge_send.at[at]).start()
-
-    @pl.when(passes)
-    def _():
-        passed(block(me), me).start()
-
-    @pl.loop(0, peers - 1)
-    def _(i):
-        device = lax.rem(me + peers - offset_of(i), peers)
-        arriving(device).wait_recv()
-
-        @pl.when(passes)
-        def _():
-            passed(first.at[rows(device)], device).start()
+        @pl.when(i < peers - 1)
+        def _():
+            sent(lax.rem(me + offset_of(i), peers)).start()
+
+        for at, edge in enumerate(edges):
+            to = device_at(group, edge - 1)
+            due = i == (at + 1) * (peers - 1) // (len(edges) + 1)
+
+            @pl.when(jnp.logical_and(due, to != me))
+            def _():
+                edged(at, edge, to).start()
+
+            @pl.when(jnp.logical_and(due, to == me))
+            def _():
+                pltpu.make_async_copy(block_at(edge), second.at[rows(me)], edge_send.at[at]).start()
+
+        @pl.when(i >= WINDOW)
+        def _():
+            away = offset_of(i - WINDOW)
+            device = lax.rem(me + peers - away, peers)
+            sent(lax.rem(me + away, peers)).wait_send()
+            arriving(device).wait_recv()
+
+            @pl.when(passes)
+            def _():
+                passed(first.at[rows(device)], device).start()
 
     own.wait()
-
-    @pl.loop(1, peers)
-    def _(i):
-        sent(lax.rem(me + i, peers)).wait_send()
 
     @pl.when(passes)
     def _():
@@ -541,32 +545,35 @@
 
     greet(group, me, place)
 
-    @pl.when(has_next)
-    def _():
-        @pl.loop(0, peers - 1)
-        def _(i):
+    own = pltpu.make_async_copy(total.at[rows(me)], block(me), local)
+
+    @pl.loop(0, peers + AHEAD)
+    def _(i):
+        @pl.when(jnp.logical_and(has_next, i < peers))
+        def _():
             passed(lax.rem(after["chan"] + offset_of(i), peers)).start()
 
-        passed(after["chan"]).start()
-
-    @pl.loop(0, peers - 1)
-    def _(i):
-        device = lax.rem(me + offset_of(i), peers)
-        add(device)
-        sent(device).start()
+        @pl.when(jnp.logical_and(i >= AHEAD, i < peers - 1 + AHEAD))
+        def _():
+            device = lax.rem(me + offset_of(i - AHEAD), peers)
+            add(device)
+            sent(device).start()
+
+        @pl.when(jnp.logical_and(i >= AHEAD + WINDOW, i < peers - 1 + AHEAD))
+        def _():
+            sent(lax.rem(me + offset_of(i - AHEAD - WINDOW), peers)).wait_send()
 
     add(me)
-    own = pltpu.make_async_copy(total.at[rows(me)], block(me), local)
     own.start()
     own.wait()
+
+    @pl.loop(max(peers - 1 - WINDOW, 0), peers - 1)
+    def _(i):
+        sent(lax.rem(me + offset_of(i), peers)).wait_send()
 
     @pl.loop(1, peers)
     def _(i):
         arriving(lax.rem(me + peers - i, peers)).wait_recv()
-
-    @pl.loop(1, peers)
-    def _(i):
-        sent(lax.rem(me + i, peers)).wait_send()
 
     @pl.when(has_next)
     def _():

time: 377 us -> 380 us (level)
  transfers between devices with their start and end apart: 1 -> 1, of which waited for: 0 -> 0; matrix products, arithmetic and copies ran while one was open for 0% -> 0% of each run, Pallas kernels for 39% -> 40%
where the time goes in v5:
time: 380 us; the launch traced here: 377 us
  Pallas kernels  349 us (92%)
  between operations  13.4 us (4%)
  other arithmetic  7.75 us (2%)
  local copies, waits for them, and re-layouts  6.86 us (2%)
    pallas_call x1, Pallas kernels, gather_frames(): pl.pallas_call(gather_kernel, out_shape=(half, half), in_specs=[anywhere]...  150 us
    pallas_call x1, Pallas kernels, scatter_frames(): pl.pallas_call(scatter_kernel, out_shape=jax.ShapeDtypeStruct((channels,...  149 us
    pallas_call x1, Pallas kernels, filter_frame(): pl.pallas_call(frame_kernel, out_shape=(half, half), in_specs=[whole] * (...  49.6 us
  transfers between devices with their start and end apart: 1, of which 0 were waited for; matrix products, arithmetic and copies ran while one was open for 0% of the time, Pallas kernels for 40%

profile of v5, /device:TPU:15, one launch (start us, length us, event | category | flops | bytes accessed | tf_op | source)
XLA Modules:
  0.0 376.6 jit_solution(9202769231202157208)
XLA Ops:
  6.5 0.0 copy-start.1
  6.5 0.0 all-gather.2.cloned.1.call-start
  6.5 1.1 convert_element_type.6
  7.6 0.5 reshape.6
  8.2 0.2 copy.13
  8.4 0.9 copy.16
  9.3 0.0 all-gather.2.cloned.1.call-update
  9.3 0.0 copy-start
  9.3 150.0 %shard_map.109 = (bf16[8192,256]{1,0:T(8,128)(2,1)}, bf16[8192,256]{1,0:T(8,128)(2,1)}) custom-call(bf16[512,4096]{1,0:T(8,128)(2,1)} %record.1), custom_call_target="tpu_custom_call" | custom-call | bytes 300000000 | tf_op jit(solution)/shard_map/pallas_call | solution.py:593
  159.3 0.0 all-gather.2.cloned.1.call-done.gate
  159.3 0.0 copy-done.1
  159.3 2.6 jit_solution_.6.tw_cos
  162.0 0.0 copy-done
  162.0 2.6 jit_solution_.7.tw_sin
  164.5 49.6 %shard_map.110 = (bf16[8192,256]{1,0:T(8,128)(2,1)}, bf16[8192,256]{1,0:T(8,128)(2,1)}) custom-call(bf16[8192,256]{1,0:T(8,128)(2,1)} %get-tuple-element.9.first, bf16[8192,256]{1,0:T(8,128)(2,1)} %get-tuple-element.10.second, f32[1,512]{1,0:T(1,128)} %constant.18.clone.taper, bf16[2,512,256]{2,1,0:T(8,128)(2,1)} %constant.19.clone.fwd_time, ...), custom_call_target="tpu_custom_call" | custom-call | flops 16000000000 | bytes 30000000 | tf_op jit(solution)/shard_map/pallas_call | solution.py:283
  214.1 149.0 %shard_map.111 = bf16[512,4096]{1,0:T(8,128)(2,1)} custom-call(bf16[8192,256]{1,0:T(8,128)(2,1)} %get-tuple-element.11.head, bf16[8192,256]{1,0:T(8,128)(2,1)} %get-tuple-element.12.tail), custom_call_target="tpu_custom_call" | custom-call | bytes 300000000 | tf_op jit(solution)/shard_map/pallas_call | solution.py:609
  363.1 6.7 %convert_element_type.7 = f32[512,4096]{1,0:T(8,128)} convert(bf16[512,4096]{1,0:T(8,128)(2,1)} %shard_map.111) | non-fusion elementwise | flops 2097152 | bytes 12582912 | tf_op jit(solution)/shard_map/convert_element_type | solution.py:630
Async XLA Ops:
  6.5 152.8 %copy-start.1 = (f32[8192]{0:T(1024)S(1)}, f32[8192]{0:T(1024)}, u32[]{:S(2)}) copy-start(f32[8192]{0:T(1024)} %constant.25.clone) | copy-start | bytes 98308
  6.5 152.8 %all-gather.2.cloned.1.call-start = ((), (), s32[]{:S(2)}) async-start(), calls=%async_computation | async-start | bytes 4456448 | tf_op jit(solution)/shard_map/all_gather | solution.py:627
  9.3 152.7 %copy-start = (f32[8192]{0:T(1024)S(1)}, f32[8192]{0:T(1024)}, u32[]{:S(2)}) copy-start(f32[8192]{0:T(1024)} %constant.26.clone) | copy-start | bytes 98308
Sparse Core Ops, SparseCore 0:
  9.5 94.6 all-gather.1

commit v6 on v5

--- a/solution.py
+++ b/solution.py
@@ -364,8 +364,8 @@
 
 
 EDGE = 4
-WINDOW = 5
-AHEAD = 3
+WINDOW = 8
+AHEAD = 4
 
 
 def edge_places():
@@ -377,7 +377,7 @@
     groups, peers = lax.axis_size("tm"), lax.axis_size("chan")
     group, me = lax.axis_index("tm"), lax.axis_index("chan")
     place = place_of(group, me)
-    size = record.shape[0]
+    size = record.shape[1]
     has_prev = jnp.logical_or(place > 0, group > 0)
     has_next = jnp.logical_or(place < peers - 1, group < groups - 1)
 
@@ -390,7 +390,7 @@
         return pl.ds(pl.multiple_of(device * size, size), size)
 
     def block_at(spot):
-        return record.at[:, pl.ds(pl.multiple_of(spot * HOP, HOP), HOP)]
+        return record.at[spot]
 
     def block(device):
         return block_at(place_of(group, device))
@@ -501,7 +501,7 @@
     groups, peers = lax.axis_size("tm"), lax.axis_size("chan")
     group, me = lax.axis_index("tm"), lax.axis_index("chan")
     place = place_of(group, me)
-    size = out.shape[0]
+    size = out.shape[1]
     has_prev = jnp.logical_or(place > 0, group > 0)
     has_next = jnp.logical_or(place < peers - 1, group < groups - 1)
     after = along_line(group, place, 1)
@@ -510,7 +510,7 @@
         return pl.ds(pl.multiple_of(device * size, size), size)
 
     def block(device):
-        return out.at[:, pl.ds(pl.multiple_of(place_of(group, device) * HOP, HOP), HOP)]
+        return out.at[place_of(group, device)]
 
     def passed(device):
         return remote(
@@ -595,7 +595,7 @@
         out_shape=(half, half),
         in_specs=[anywhere],
         out_specs=(anywhere, anywhere),
-        scratch_shapes=[pltpu.VMEM((record.shape[0], HOP), record.dtype)] + exchange_scratch()
+        scratch_shapes=[pltpu.VMEM(record.shape[1:], record.dtype)] + exchange_scratch()
         + [pltpu.SemaphoreType.DMA((max(len(edge_places()), 1),))],
         compiler_params=pltpu.CompilerParams(
             collective_id=0, has_side_effects=True, vmem_limit_bytes=60 * 1024 * 1024
@@ -604,11 +604,12 @@
     )(record)
 
 
-def scatter_frames(head, tail, channels, span_len):
+def scatter_frames(head, tail, channels):
+    peers = lax.axis_size("chan")
     anywhere = pl.BlockSpec(memory_space=pl.ANY)
     return pl.pallas_call(
         scatter_kernel,
-        out_shape=jax.ShapeDtypeStruct((channels, span_len), head.dtype),
+        out_shape=jax.ShapeDtypeStruct((peers, channels, HOP), head.dtype),
         in_specs=[pl.BlockSpec(memory_space=pltpu.VMEM), anywhere],
         out_specs=anywhere,
         scratch_shapes=[pltpu.VMEM((NCH, HOP), head.dtype)] * 2 + exchange_scratch(),
@@ -625,9 +626,11 @@
     gate = fan_mask.astype(jnp.bfloat16).reshape(local_bins, SECTION_B, SECTION_A)
     gate = gate.transpose(0, 2, 1).reshape(local_bins, NCH)
     gate = lax.all_gather(gate, "chan", axis=0, tiled=True)
-    first, second = gather_frames(record)
+    pieces = record.reshape(channels, span_len // HOP, HOP).transpose(1, 0, 2)
+    first, second = gather_frames(pieces)
     head, tail = filter_frame(first, second, frame_tables(), gate)
-    return scatter_frames(head, tail, channels, span_len).astype(jnp.float32)
+    pieces = scatter_frames(head, tail, channels).astype(jnp.float32)
+    return pieces.transpose(1, 0, 2).reshape(channels, span_len)
 
 
 def body(record, fan_mask):

time: 380 us -> 407 us (1.071)
  local copies, waits for them, and re-layouts: 6.86 us -> 37.8 us
  Pallas kernels: 349 us -> 343 us
    reshape x0 -> x3, local copies, waits for them, and re-layouts: none -> 24.6 us  [the longest x2 18.2 us: frames_body(): return pieces.transpose(1, 0, 2).reshape(channels, span_len)]
    convert_element_type x1 -> x0, other arithmetic: 6.67 us -> none  [frames_body(): return scatter_frames(head, tail, channels, span_len).astype(jnp.float32)]
    reshape x0 -> x1, other arithmetic: none -> 6.49 us  [frames_body(): return pieces.transpose(1, 0, 2).reshape(channels, span_len)]
    unnamed x5 -> x6, local copies, waits for them, and re-layouts: 0.89 us -> 7.3 us
    pallas_call x1, Pallas kernels: 150 us -> 144 us  [gather_frames(): pl.pallas_call(gather_kernel, out_shape=(half, half), in_specs=[anywhere]...]
  transfers between devices with their start and end apart: 1 -> 1, of which waited for: 0 -> 0; matrix products, arithmetic and copies ran while one was open for 0% -> 3% of each run, Pallas kernels for 40% -> 36%
where the time goes in v6:
time: 407 us; the launch traced here: 402 us
  Pallas kernels  343 us (84%)
  local copies, waits for them, and re-layouts  37.8 us (9%)
  between operations  13.4 us (3%)
  other arithmetic  7.56 us (2%)
    pallas_call x1, Pallas kernels, scatter_frames(): pl.pallas_call(scatter_kernel, out_shape=jax.ShapeDtypeStruct((peers, cha...  150 us
    pallas_call x1, Pallas kernels, gather_frames(): pl.pallas_call(gather_kernel, out_shape=(half, half), in_specs=[anywhere]...  144 us
    pallas_call x1, Pallas kernels, filter_frame(): pl.pallas_call(frame_kernel, out_shape=(half, half), in_specs=[whole] * (...  49.6 us
    reshape x2, local copies, waits for them, and re-layouts, frames_body(): return pieces.transpose(1, 0, 2).reshape(channels, span_len)  18.2 us
  transfers between devices with their start and end apart: 1, of which 0 were waited for; matrix products, arithmetic and copies ran while one was open for 3% of the time, Pallas kernels for 36%

profile of v6, /device:TPU:15, one launch (start us, length us, event | category | flops | bytes accessed | tf_op | source)
XLA Modules:
  0.0 402.0 jit_solution(4204044995037961994)
XLA Ops:
  6.5 0.0 all-gather.2.cloned.1.call-start
  6.5 1.1 convert_element_type.4
  7.6 0.5 reshape.16
  8.2 0.2 copy.15
  8.4 0.9 copy.20
  9.3 0.0 all-gather.2.cloned.1.call-update
  9.3 6.4 %copy.13 = bf16[512,4096]{0,1:T(8,128)(2,1)} copy(bf16[512,4096]{1,0:T(8,128)(2,1)} %param.11) | data formatting | bytes 8388608 | tf_op args[0]
  15.7 6.4 %copy.14 = bf16[512,16,256]{2,0,1:T(8,128)(2,1)} copy(bf16[512,16,256]{0,2,1:T(8,128)(2,1)} %bitcast.12) | data formatting | bytes 8388608 | tf_op jit(solution)/shard_map/reshape | solution.py:629
  22.1 0.0 copy-start.1
  22.1 0.0 copy-start
  22.1 144.0 %shard_map.109 = (bf16[8192,256]{1,0:T(8,128)(2,1)}, bf16[8192,256]{1,0:T(8,128)(2,1)}) custom-call(bf16[16,512,256]{2,1,0:T(8,128)(2,1)} %bitcast.11), custom_call_target="tpu_custom_call" | custom-call | bytes 300000000 | tf_op jit(solution)/shard_map/pallas_call | solution.py:593
  166.1 0.0 all-gather.2.cloned.1.call-done.gate
  166.1 0.0 copy-done.1
  166.1 2.6 jit_solution_.6.tw_cos
  168.8 0.0 copy-done
  168.8 2.6 jit_solution_.7.tw_sin
  171.3 49.6 %shard_map.110 = (bf16[8192,256]{1,0:T(8,128)(2,1)}, bf16[8192,256]{1,0:T(8,128)(2,1)}) custom-call(bf16[8192,256]{1,0:T(8,128)(2,1)} %get-tuple-element.9.first, bf16[8192,256]{1,0:T(8,128)(2,1)} %get-tuple-element.10.second, f32[1,512]{1,0:T(1,128)} %constant.18.clone.taper, bf16[2,512,256]{2,1,0:T(8,128)(2,1)} %constant.19.clone.fwd_time, ...), custom_call_target="tpu_custom_call" | custom-call | flops 16000000000 | bytes 30000000 | tf_op jit(solution)/shard_map/pallas_call | solution.py:283
  220.9 149.6 %shard_map.111 = bf16[16,512,256]{2,1,0:T(8,128)(2,1)} custom-call(bf16[8192,256]{1,0:T(8,128)(2,1)} %get-tuple-element.11.head, bf16[8192,256]{1,0:T(8,128)(2,1)} %get-tuple-element.12.tail), custom_call_target="tpu_custom_call" | custom-call | bytes 300000000 | tf_op jit(solution)/shard_map/pallas_call | solution.py:610
  370.5 6.5 %convert_bitcast_fusion = f32[512,16,256]{2,0,1:T(8,128)} fusion(bf16[16,512,256]{2,1,0:T(8,128)(2,1)} %shard_map.111), kind=kLoop, calls=%fused_computation | loop fusion | flops 2097152 | bytes 12582912 | tf_op jit(solution)/shard_map/reshape | solution.py:633
  377.0 9.3 %copy.16 = f32[512,16,256]{0,2,1:T(8,128)} copy(f32[512,16,256]{2,0,1:T(8,128)} %convert_bitcast_fusion) | data formatting | bytes 16777216 | tf_op jit(solution)/shard_map/reshape | solution.py:633
  386.3 8.9 %copy.17 = f32[512,4096]{1,0:T(8,128)} copy(f32[512,4096]{0,1:T(8,128)} %bitcast.10) | data formatting | bytes 16777216 | tf_op jit(solution)/shard_map/reshape | solution.py:633
Async XLA Ops:
  6.5 159.6 %all-gather.2.cloned.1.call-start = ((), (), s32[]{:S(2)}) async-start(), calls=%async_computation | async-start | bytes 4456448 | tf_op jit(solution)/shard_map/all_gather | solution.py:628
  22.1 144.0 %copy-start.1 = (f32[8192]{0:T(1024)S(1)}, f32[8192]{0:T(1024)}, u32[]{:S(2)}) copy-start(f32[8192]{0:T(1024)} %constant.25.clone) | copy-start | bytes 98308
  22.1 146.7 %copy-start = (f32[8192]{0:T(1024)S(1)}, f32[8192]{0:T(1024)}, u32[]{:S(2)}) copy-start(f32[8192]{0:T(1024)} %constant.26.clone) | copy-start | bytes 98308
Sparse Core Ops, SparseCore 0:
  9.5 101.6 all-gather.1

commit v7 on v4

--- a/solution.py
+++ b/solution.py
@@ -362,7 +362,7 @@
     )
 
 
-EDGE = 4
+EDGE = 2
 
 
 def edge_places():

time: 377 us -> 385 us (1.021)
  Pallas kernels: 347 us -> 357 us
    pallas_call x1, Pallas kernels: 146 us -> 164 us  [gather_frames(): pl.pallas_call(gather_kernel, out_shape=(half, half), in_specs=[anywhere]...]
    pallas_call x1, Pallas kernels: 151 us -> 143 us  [scatter_frames(): pl.pallas_call(scatter_kernel, out_shape=jax.ShapeDtypeStruct((channels,...]
  transfers between devices with their start and end apart: 1 -> 1, of which waited for: 0 -> 0; matrix products, arithmetic and copies ran while one was open for 0% -> 0% of each run, Pallas kernels for 39% -> 43%
where the time goes in v7:
time: 385 us
  Pallas kernels  357 us (93%)
  between operations  13.4 us (3%)
  other arithmetic  7.75 us (2%)
  local copies, waits for them, and re-layouts  6.86 us (2%)
    pallas_call x1, Pallas kernels, gather_frames(): pl.pallas_call(gather_kernel, out_shape=(half, half), in_specs=[anywhere]...  164 us
    pallas_call x1, Pallas kernels, scatter_frames(): pl.pallas_call(scatter_kernel, out_shape=jax.ShapeDtypeStruct((channels,...  143 us
    pallas_call x1, Pallas kernels, filter_frame(): pl.pallas_call(frame_kernel, out_shape=(half, half), in_specs=[whole] * (...  49.6 us
  transfers between devices with their start and end apart: 1, of which 0 were waited for; matrix products, arithmetic and copies ran while one was open for 0% of the time, Pallas kernels for 43%

profile of v7, /device:TPU:15, one launch (start us, length us, event | category | flops | bytes accessed | tf_op | source)
XLA Modules:
  0.0 385.1 jit_solution(9878904699742638016)
XLA Ops:
  6.5 0.0 copy-start.1
  6.5 0.0 all-gather.2.cloned.1.call-start
  6.5 1.1 convert_element_type.6
  7.6 0.5 reshape.6
  8.2 0.2 copy.13
  8.4 0.9 copy.16
  9.3 0.0 all-gather.2.cloned.1.call-update
  9.3 0.0 copy-start
  9.3 164.3 %shard_map.109 = (bf16[8192,256]{1,0:T(8,128)(2,1)}, bf16[8192,256]{1,0:T(8,128)(2,1)}) custom-call(bf16[512,4096]{1,0:T(8,128)(2,1)} %record.1), custom_call_target="tpu_custom_call" | custom-call | bytes 300000000 | tf_op jit(solution)/shard_map/pallas_call | solution.py:586
  173.6 0.0 all-gather.2.cloned.1.call-done.gate
  173.6 0.0 copy-done.1
  173.6 2.6 jit_solution_.6.tw_cos
  176.3 0.0 copy-done
  176.3 2.6 jit_solution_.7.tw_sin
  178.9 49.6 %shard_map.110 = (bf16[8192,256]{1,0:T(8,128)(2,1)}, bf16[8192,256]{1,0:T(8,128)(2,1)}) custom-call(bf16[8192,256]{1,0:T(8,128)(2,1)} %get-tuple-element.9.first, bf16[8192,256]{1,0:T(8,128)(2,1)} %get-tuple-element.10.second, f32[1,512]{1,0:T(1,128)} %constant.18.clone.taper, bf16[2,512,256]{2,1,0:T(8,128)(2,1)} %constant.19.clone.fwd_time, ...), custom_call_target="tpu_custom_call" | custom-call | flops 16000000000 | bytes 30000000 | tf_op jit(solution)/shard_map/pallas_call | solution.py:283
  228.5 143.1 %shard_map.111 = bf16[512,4096]{1,0:T(8,128)(2,1)} custom-call(bf16[8192,256]{1,0:T(8,128)(2,1)} %get-tuple-element.11.head, bf16[8192,256]{1,0:T(8,128)(2,1)} %get-tuple-element.12.tail), custom_call_target="tpu_custom_call" | custom-call | bytes 300000000 | tf_op jit(solution)/shard_map/pallas_call | solution.py:602
  371.6 6.7 %convert_element_type.7 = f32[512,4096]{1,0:T(8,128)} convert(bf16[512,4096]{1,0:T(8,128)(2,1)} %shard_map.111) | non-fusion elementwise | flops 2097152 | bytes 12582912 | tf_op jit(solution)/shard_map/convert_element_type | solution.py:623
Async XLA Ops:
  6.5 167.1 %copy-start.1 = (f32[8192]{0:T(1024)S(1)}, f32[8192]{0:T(1024)}, u32[]{:S(2)}) copy-start(f32[8192]{0:T(1024)} %constant.25.clone) | copy-start | bytes 98308
  6.5 167.1 %all-gather.2.cloned.1.call-start = ((), (), s32[]{:S(2)}) async-start(), calls=%async_computation | async-start | bytes 4456448 | tf_op jit(solution)/shard_map/all_gather | solution.py:620
  9.3 167.0 %copy-start = (f32[8192]{0:T(1024)S(1)}, f32[8192]{0:T(1024)}, u32[]{:S(2)}) copy-start(f32[8192]{0:T(1024)} %constant.26.clone) | copy-start | bytes 98308
Sparse Core Ops, SparseCore 0:
  9.5 110.6 all-gather.1

commit v8 on v4

--- a/solution.py
+++ b/solution.py
@@ -363,6 +363,8 @@
 
 
 EDGE = 4
+WINDOW = 5
+AHEAD = 3
 
 
 def edge_places():
@@ -541,32 +543,35 @@
 
     greet(group, me, place)
 
-    @pl.when(has_next)
-    def _():
-        @pl.loop(0, peers - 1)
-        def _(i):
+    own = pltpu.make_async_copy(total.at[rows(me)], block(me), local)
+
+    @pl.loop(0, peers + AHEAD)
+    def _(i):
+        @pl.when(jnp.logical_and(has_next, i < peers))
+        def _():
             passed(lax.rem(after["chan"] + offset_of(i), peers)).start()
 
-        passed(after["chan"]).start()
-
-    @pl.loop(0, peers - 1)
-    def _(i):
-        device = lax.rem(me + offset_of(i), peers)
-        add(device)
-        sent(device).start()
+        @pl.when(jnp.logical_and(i >= AHEAD, i < peers - 1 + AHEAD))
+        def _():
+            device = lax.rem(me + offset_of(i - AHEAD), peers)
+            add(device)
+            sent(device).start()
+
+        @pl.when(jnp.logical_and(i >= AHEAD + WINDOW, i < peers - 1 + AHEAD))
+        def _():
+            sent(lax.rem(me + offset_of(i - AHEAD - WINDOW), peers)).wait_send()
 
     add(me)
-    own = pltpu.make_async_copy(total.at[rows(me)], block(me), local)
     own.start()
     own.wait()
+
+    @pl.loop(max(peers - 1 - WINDOW, 0), peers - 1)
+    def _(i):
+        sent(lax.rem(me + offset_of(i), peers)).wait_send()
 
     @pl.loop(1, peers)
     def _(i):
         arriving(lax.rem(me + peers - i, peers)).wait_recv()
-
-    @pl.loop(1, peers)
-    def _(i):
-        sent(lax.rem(me + i, peers)).wait_send()
 
     @pl.when(has_next)
     def _():

time: 377 us -> 380 us (level)
  no operation moved by 1% of the time
where the time goes in v8:
time: 380 us; the launch traced here: 375 us
  Pallas kernels  347 us (91%)
  between operations  13.4 us (4%)
  other arithmetic  7.75 us (2%)
  local copies, waits for them, and re-layouts  6.86 us (2%)
    pallas_call x1, Pallas kernels, scatter_frames(): pl.pallas_call(scatter_kernel, out_shape=jax.ShapeDtypeStruct((channels,...  151 us
    pallas_call x1, Pallas kernels, gather_frames(): pl.pallas_call(gather_kernel, out_shape=(half, half), in_specs=[anywhere]...  146 us
    pallas_call x1, Pallas kernels, filter_frame(): pl.pallas_call(frame_kernel, out_shape=(half, half), in_specs=[whole] * (...  49.6 us
  transfers between devices with their start and end apart: 1, of which 0 were waited for; matrix products, arithmetic and copies ran while one was open for 0% of the time, Pallas kernels for 39%

profile of v8, /device:TPU:15, one launch (start us, length us, event | category | flops | bytes accessed | tf_op | source)
XLA Modules:
  0.0 375.4 jit_solution(13311978323570153822)
XLA Ops:
  6.5 0.0 copy-start.1
  6.5 0.0 all-gather.2.cloned.1.call-start
  6.5 1.1 convert_element_type.6
  7.6 0.5 reshape.6
  8.2 0.2 copy.13
  8.4 0.9 copy.16
  9.3 0.0 all-gather.2.cloned.1.call-update
  9.3 0.0 copy-start
  9.3 146.5 %shard_map.109 = (bf16[8192,256]{1,0:T(8,128)(2,1)}, bf16[8192,256]{1,0:T(8,128)(2,1)}) custom-call(bf16[512,4096]{1,0:T(8,128)(2,1)} %record.1), custom_call_target="tpu_custom_call" | custom-call | bytes 300000000 | tf_op jit(solution)/shard_map/pallas_call | solution.py:591
  155.8 0.0 all-gather.2.cloned.1.call-done.gate
  155.8 0.0 copy-done.1
  155.8 2.6 jit_solution_.6.tw_cos
  158.5 0.0 copy-done
  158.5 2.6 jit_solution_.7.tw_sin
  161.1 49.6 %shard_map.110 = (bf16[8192,256]{1,0:T(8,128)(2,1)}, bf16[8192,256]{1,0:T(8,128)(2,1)}) custom-call(bf16[8192,256]{1,0:T(8,128)(2,1)} %get-tuple-element.9.first, bf16[8192,256]{1,0:T(8,128)(2,1)} %get-tuple-element.10.second, f32[1,512]{1,0:T(1,128)} %constant.18.clone.taper, bf16[2,512,256]{2,1,0:T(8,128)(2,1)} %constant.19.clone.fwd_time, ...), custom_call_target="tpu_custom_call" | custom-call | flops 16000000000 | bytes 30000000 | tf_op jit(solution)/shard_map/pallas_call | solution.py:283
  210.7 151.2 %shard_map.111 = bf16[512,4096]{1,0:T(8,128)(2,1)} custom-call(bf16[8192,256]{1,0:T(8,128)(2,1)} %get-tuple-element.11.head, bf16[8192,256]{1,0:T(8,128)(2,1)} %get-tuple-element.12.tail), custom_call_target="tpu_custom_call" | custom-call | bytes 300000000 | tf_op jit(solution)/shard_map/pallas_call | solution.py:607
  361.9 6.7 %convert_element_type.7 = f32[512,4096]{1,0:T(8,128)} convert(bf16[512,4096]{1,0:T(8,128)(2,1)} %shard_map.111) | non-fusion elementwise | flops 2097152 | bytes 12582912 | tf_op jit(solution)/shard_map/convert_element_type | solution.py:628
Async XLA Ops:
  6.5 149.3 %copy-start.1 = (f32[8192]{0:T(1024)S(1)}, f32[8192]{0:T(1024)}, u32[]{:S(2)}) copy-start(f32[8192]{0:T(1024)} %constant.25.clone) | copy-start | bytes 98308
  6.5 149.3 %all-gather.2.cloned.1.call-start = ((), (), s32[]{:S(2)}) async-start(), calls=%async_computation | async-start | bytes 4456448 | tf_op jit(solution)/shard_map/all_gather | solution.py:625
  9.3 149.2 %copy-start = (f32[8192]{0:T(1024)S(1)}, f32[8192]{0:T(1024)}, u32[]{:S(2)}) copy-start(f32[8192]{0:T(1024)} %constant.26.clone) | copy-start | bytes 98308
Sparse Core Ops, SparseCore 0:
  9.5 110.5 all-gather.1
